TPU v7x, 128 devices: a whole 4x4x4 slice. The times are simulated.
128 devices in a mesh: seq: 8 (over z, core), head: 16 (over x, y).
Axes of the slice: x: 4, y: 4, z: 4, core: 2. Of those that a mesh axis runs over, the one named last changes fastest.
Arguments:
- tokens: bfloat16 [16384, 2048], P(('seq', 'head')), may hold values from -6 to 6
- doc_starts: int32 [8, 3], P('seq'), may hold values from 0 to 127, as said below
- norm_gain: float32 [2048], replicated, may hold values from 0.5 to 1.5
- w_in: bfloat16 [2048, 4, 2048], P(None, None, 'head'), may hold values from -0.125 to 0.125
- w_rate: bfloat16 [2048, 32], P(None, 'head'), may hold values from -0.125 to 0.125
- rate_bias: float32 [32], P('head'), may hold values from -2 to 2
- ttt_w: float32 [32, 64, 64], P('head'), may hold values from -0.75 to 0.75
- ttt_b: float32 [32, 64], P('head'), may hold values from -2 to 2
- ttt_gain: float32 [32, 64], P('head'), may hold values from 0.25 to 1.75
- ttt_shift: float32 [32, 64], P('head'), may hold values from -2 to 2
- post_gain: float32 [2048], P('head'), may hold values from 0.25 to 1.75
- post_bias: float32 [2048], P('head'), may hold values from -2 to 2
- w_out: bfloat16 [2048, 2048], P('head'), may hold values from -0.25 to 0.25
- ffn_gain: float32 [2048], replicated, may hold values from 0.5 to 1.5
- w_gate_up: bfloat16 [2048, 2, 5504], P(None, None, 'head'), may hold values from -0.125 to 0.125
- w_down: bfloat16 [5504, 2048], P('head'), may hold values from -0.15625 to 0.15625
- cotangent: bfloat16 [16384, 2048], P(('seq', 'head')), may hold values from -6 to 6
Outputs:
- output: bfloat16 [16384, 2048], P(('seq', 'head'))
- grad_tokens: float32 [16384, 2048], P(('seq', 'head'))
- grad_norm_gain: float32 [2048], replicated
- grad_w_in: float32 [2048, 4, 2048], P(None, None, 'head')
- grad_w_rate: float32 [2048, 32], P(None, 'head')
- grad_rate_bias: float32 [32], P('head')
- grad_ttt_w: float32 [32, 64, 64], P('head')
- grad_ttt_b: float32 [32, 64], P('head')
- grad_ttt_gain: float32 [32, 64], P('head')
- grad_ttt_shift: float32 [32, 64], P('head')
- grad_post_gain: float32 [2048], P('head')
- grad_post_bias: float32 [2048], P('head')
- grad_w_out: float32 [2048, 2048], P('head')
- grad_ffn_gain: float32 [2048], replicated
- grad_w_gate_up: float32 [2048, 2, 5504], P(None, None, 'head')
- grad_w_down: float32 [5504, 2048], P('head')
Inputs may be any that keep to these rules, and one draw needn't show every extreme that they name: `doc_starts`: in each row the three starts increase; the first is 0, the second lies in 1 to 7 and the third in 121 to 127; in some row the third is 127.
All inputs are finite; a program needn't handle non-finite values.
Results may differ from a plain program's by a relative error of at most 0.025.
Values may be sent and summed in bfloat16 or wider, within the bound.
A program may use at most 192 MiB of HBM per device.

v0:
```python
from functools import partial

import jax
import jax.numpy as jnp
from jax import lax
from jax.experimental import pallas as pl
from jax.experimental.pallas import tpu as pltpu
from jax.sharding import PartitionSpec as P

MB = 16
EPS = 1e-06
HD = 64
STEPS = 4
CHUNK = STEPS * MB
LANES = 2 * CHUNK
BF16 = jnp.bfloat16
F32 = jnp.float32


def dot_nn(a, b):
    return lax.dot_general(a, b, (((1,), (0,)), ((), ())), preferred_element_type=F32)


def dot_nt(a, b):
    return lax.dot_general(a, b, (((1,), (1,)), ((), ())), preferred_element_type=F32)


def dot_tn(a, b):
    return lax.dot_general(a, b, (((0,), (0,)), ((), ())), preferred_element_type=F32)


def sum_rows(x):
    return jnp.sum(x, axis=0, keepdims=True)


def square_iota(dim):
    return lax.broadcasted_iota(jnp.int32, (LANES, LANES), dim)


def step_of(index):
    return (index >> 4) & (STEPS - 1)


class Places:
    def __init__(self, starts_ref):
        self.second = starts_ref[0, 1]
        self.third = starts_ref[0, 2]

    def document(self, step):
        return (step >= self.second).astype(jnp.int32) + (step >= self.third).astype(jnp.int32)

    def lane_documents(self, chunk):
        return self.document(chunk * STEPS + step_of(lax.broadcasted_iota(jnp.int32, (1, LANES), 1)))

    def row_documents(self, chunk):
        return self.document(chunk * STEPS + step_of(lax.broadcasted_iota(jnp.int32, (LANES, 1), 0)))

    def entry(self, chunk):
        return self.document(chunk * STEPS - 1)

    def last(self, chunk):
        return self.document(chunk * STEPS + STEPS - 1)

    def keeps(self, chunk):
        return (self.entry(chunk) == self.last(chunk)).astype(F32)


def split_heads(rows):
    first = lax.broadcasted_iota(jnp.int32, rows.shape, 1) < HD
    zero = jnp.zeros_like(rows)
    return jnp.concatenate([jnp.where(first, rows, zero), jnp.where(first, zero, rows)], axis=0)


def join_heads(square):
    first = lax.broadcasted_iota(jnp.int32, (CHUNK, LANES), 1) < HD
    return jnp.where(first, square[:CHUNK], square[CHUNK:])


def to_columns(rows):
    turned = split_heads(rows).T
    return turned[:HD] + turned[HD:]


def to_rows(columns):
    return join_heads(split_heads(columns).T)


def selector():
    row = lax.broadcasted_iota(jnp.int32, (HD, LANES), 0)
    col = lax.broadcasted_iota(jnp.int32, (HD, LANES), 1)
    return (row == (col & (HD - 1))).astype(F32).astype(BF16)


RING = 4


def slot(chunk):
    return lax.rem(chunk, RING)


def wrap(chunk, chunks):
    return lax.rem(chunk + chunks, chunks)


def chunk_rows(chunk):
    return pl.ds(pl.multiple_of(chunk * CHUNK, CHUNK), CHUNK)


def same_head():
    return (square_iota(0) >> 6) == (square_iota(1) >> 6)


def masked(values, keep):
    return jnp.where(keep, values, jnp.zeros_like(values))


def inner_masks(head_ref, earlier_ref, output_ref):
    row, col = square_iota(0), square_iota(1)
    same = same_head()
    step_row, step_col = step_of(row), step_of(col)
    earlier = jnp.where(same & (step_row < step_col), 1.0, 0.0)
    place = (col & (MB - 1)).astype(F32)
    within = jnp.where(
        same & (step_row == step_col) & ((row & (MB - 1)) <= (col & (MB - 1))),
        MB / (place + 1.0),
        0.0,
    )
    head_ref[...] = jnp.where(same, 1.0, 0.0)
    earlier_ref[...] = earlier
    output_ref[...] = earlier + within


def centred_columns(values):
    return values - sum_rows(values) / HD


def spread(pairs):
    return jnp.concatenate(
        [jnp.broadcast_to(pairs[h : h + 1], (HD, HD)) for h in range(2)], axis=0
    ).T


def forward_kernel(
    starts_ref,
    proj_ref,
    rate_ref,
    ttt_w_ref,
    ttt_b_ref,
    ttt_gain_ref,
    ttt_shift_ref,
    cot_ref,
    inner_ref,
    z_ref,
    g_ref,
    out_ref,
    target_ref,
    state_ref,
    mi_ref,
    mx_ref,
    mo_ref,
    w_ref,
    gain_ref,
    base_ref,
    offset_ref,
    cot_rows_ref,
    head_ref,
    earlier_ref,
    output_ref,
    c_ref,
    shift_ref,
    *gather_sems,
):
    chunks = rate_ref.shape[0]
    gather = Gather(cot_ref, cot_rows_ref, *gather_sems)
    gather.start()
    places = Places(starts_ref)
    inner_masks(head_ref, earlier_ref, output_ref)
    w_ref[...] = centred_columns(jnp.concatenate([ttt_w_ref[0], ttt_w_ref[1]], axis=0).T)
    c_ref[...] = centred_columns(spread(ttt_b_ref[...]))
    gain_ref[...] = spread(ttt_gain_ref[...])
    shift_ref[...] = spread(ttt_shift_ref[...])

    def columns(chunk, index):
        return proj_ref[chunk_rows(chunk), index * LANES : (index + 1) * LANES]

    def prepare(chunk):
        source = wrap(chunk, chunks)
        before = wrap(source - 1, chunks)
        keys = split_heads(columns(source, 1))
        values = split_heads(columns(source, 2))
        docs_row, docs_lane = places.row_documents(source), places.lane_documents(source)
        gram = dot_nt(keys, keys) + 1.0
        mi_ref[chunk] = masked(gram * earlier_ref[...], docs_row == docs_lane).astype(BF16)
        cross = dot_nt(split_heads(columns(before, 1)), keys) + 1.0
        mx_ref[chunk] = masked(
            cross * head_ref[...], places.row_documents(before) == docs_lane
        ).astype(BF16)
        pick = selector()
        target = dot_nt(pick, keys) - dot_nt(pick, values) + shift_ref[...]
        target_ref[chunk] = target
        offset_ref[slot(chunk)] = jnp.broadcast_to(
            sum_rows(target * gain_ref[...]) / HD, offset_ref.shape[1:]
        )

    def read_state(rows, source, weight, bias, entry):
        docs_row = places.row_documents(source)
        live_lane = places.lane_documents(source) == entry
        both = jnp.concatenate(
            [masked(rows, docs_row == entry), masked(rows, docs_row != entry)], axis=1
        )
        weights = jnp.concatenate([weight, w_ref[...]], axis=1).astype(BF16)
        return dot_nt(weights, both) + jnp.where(live_lane, bias, c_ref[...])

    def base(chunk, weight, bias, entry):
        source = wrap(chunk, chunks)
        base_ref[slot(chunk)] = read_state(split_heads(columns(source, 1)), source, weight, bias, entry)

    def chain(chunk, rated_before):
        gain = gain_ref[...]
        gain2 = gain * gain
        tied = target_ref[chunk] * gain
        tied_mean = offset_ref[slot(chunk)][0:1]
        rate = rate_ref[chunk]
        matrix = mi_ref[chunk]

        def gradient(z):
            zg = z * gain2
            s1, s2, s3, s4 = sum_rows(z * z), sum_rows(zg), sum_rows(z * zg), sum_rows(z * tied)
            rs = lax.rsqrt(s1 / HD + EPS)
            mean_g = rs * s2 / HD + tied_mean
            mean_gx = rs * (rs * s3 + s4) / HD
            return rs * (z * (rs * (gain2 - mean_gx)) + (tied - mean_g))

        first = base_ref[slot(chunk)] - dot_nn(rated_before, mx_ref[chunk])
        z = first
        g = gradient(z)
        for _ in range(STEPS - 1):
            z = first - dot_nn((g * rate).astype(BF16), matrix)
            g = gradient(z)
        z_ref[chunk] = z
        g_ref[chunk] = g
        return (g * rate).astype(BF16)

    def advance(chunk, weight, bias, rated):
        keys = split_heads(columns(chunk, 1))
        last = places.last(chunk)
        kept = places.row_documents(chunk) == last
        both = jnp.concatenate(
            [masked(keys, kept), masked(head_ref[...].astype(BF16), kept)], axis=1
        )
        step = dot_nn(rated, both)
        keep = places.keeps(chunk)
        start_w, start_c = w_ref[...], c_ref[...]
        return (
            start_w + keep * (weight - start_w) - step[:, :LANES],
            start_c + keep * (bias - start_c) - step[:, LANES:],
        )

    def finish(chunk, weight, bias, rated):
        keys = split_heads(columns(chunk, 1))
        query_rows = columns(chunk, 0)
        queries = split_heads(query_rows)
        same_doc = places.row_documents(chunk) == places.lane_documents(chunk)
        matrix = masked((dot_nt(keys, queries) + 1.0) * output_ref[...], same_doc).astype(BF16)
        mo_ref[chunk] = matrix
        out = read_state(queries, chunk, weight, bias, places.entry(chunk)) - dot_nn(rated, matrix)
        out_ref[chunk] = out
        rs = lax.rsqrt(sum_rows(out * out) / HD + EPS)
        fitted = out * rs * gain_ref[...] + shift_ref[...]
        inner_ref[chunk_rows(chunk), :] = (to_rows(fitted) + query_rows.astype(F32)).astype(BF16)

    prepare(0)
    base(0, w_ref[...], c_ref[...], places.entry(0))

    def body(chunk, carry):
        weight_before, bias_before, rated_before = carry
        for step, when in enumerate(FORWARD_STEPS):
            pl.when(chunk == when)(gather.steps[step])
        before = wrap(chunk - 1, chunks)
        weight, bias = advance(before, weight_before, bias_before, rated_before)
        state_ref[chunk] = weight
        rated = chain(chunk, rated_before)
        base(chunk + 1, weight, bias, places.entry(chunk))
        prepare(chunk + 1)
        finish(before, weight_before, bias_before, rated_before)
        return weight, bias, rated

    carry = (w_ref[...], c_ref[...], jnp.zeros((HD, LANES), BF16))
    weight, bias, rated = lax.fori_loop(0, chunks, body, carry)
    finish(chunks - 1, weight, bias, rated)
    gather.end()


FORWARD_STEPS = (5, 7, 12, 16, 20, 24, 30)
BACKWARD_STEPS = (5, 7, 10, 13, 17, 20, 24)


def backward_kernel(
    starts_ref,
    proj_ref,
    rate_ref,
    dinner_ref,
    dgate_ref,
    mix_ref,
    z_ref,
    g_ref,
    out_ref,
    target_ref,
    state_ref,
    mi_ref,
    mx_ref,
    mo_ref,
    w_ref,
    gain_ref,
    dproj_ref,
    dbias_ref,
    dw_ref,
    dc_ref,
    dgain_ref,
    dshift_ref,
    dout_ref,
    free_ref,
    base_ref,
    diag_ref,
    norm_ref,
    both_ref,
    wide_ref,
    coef_ref,
    y_ref,
    dz_ref,
    lam_ref,
    mix_rows_ref,
    head_ref,
    earlier_ref,
    output_ref,
    *gather_sems,
):
    chunks = rate_ref.shape[0]
    gather = Gather(mix_ref, mix_rows_ref, *gather_sems)
    gather.start()
    places = Places(starts_ref)
    inner_masks(head_ref, earlier_ref, output_ref)
    dbias_ref[...] = jnp.zeros_like(dbias_ref)
    dw_ref[...] = jnp.zeros_like(dw_ref)
    dc_ref[...] = jnp.zeros_like(dc_ref)
    dgain_ref[...] = jnp.zeros_like(dgain_ref)
    dshift_ref[...] = jnp.zeros_like(dshift_ref)

    def columns(chunk, index):
        return proj_ref[chunk_rows(chunk), index * LANES : (index + 1) * LANES]

    def prepare(chunk):
        gain = gain_ref[...]
        gain2 = gain * gain
        given = to_columns(dinner_ref[chunk_rows(chunk), :].astype(F32))
        out = out_ref[chunk]
        rs_out = lax.rsqrt(sum_rows(out * out) / HD + EPS)
        normal = out * rs_out
        scaled = given * gain
        dout = rs_out * (
            scaled - sum_rows(scaled) / HD - normal * (sum_rows(scaled * normal) / HD)
        )
        dgain_ref[...] += given * normal
        dshift_ref[...] += given
        rounded = dout.astype(BF16)
        dout_ref[slot(chunk)] = rounded
        free_ref[slot(chunk)] = dot_nt(rounded, mo_ref[chunk])
        z = z_ref[chunk]
        rs = lax.rsqrt(sum_rows(z * z) / HD + EPS)
        xh = z * rs
        xg = xh * gain2
        g = xg + target_ref[chunk] * gain
        mean_g = sum_rows(g) / HD
        mean_gx = sum_rows(g * xh) / HD
        mean_xg = sum_rows(xg) / HD
        diag_ref[slot(chunk)] = rs * (gain2 - mean_gx)
        norm_ref[slot(chunk)] = xh
        both_ref[slot(chunk)] = xg + g - mean_g - xh * mean_gx
        wide_ref[slot(chunk)] = xg + g
        coef_ref[slot(chunk)] = jnp.concatenate(
            [
                rs * rate_ref[chunk],
                rs,
                sum_rows(gain2) / HD + mean_gx,
                mean_xg + mean_g,
                mean_xg,
                sum_rows(xg * xh) / HD + 2.0 * mean_gx,
                jnp.zeros((2, LANES), F32),
            ],
            axis=0,
        )

    def chain(chunk, dz_after, cross):
        gain = gain_ref[...]
        gain2 = gain * gain
        diag, xh, both, wide = diag_ref[slot(chunk)], norm_ref[slot(chunk)], both_ref[slot(chunk)], wide_ref[slot(chunk)]
        coef = coef_ref[slot(chunk)]
        matrix = mi_ref[chunk]

        def pull(y):
            du = y * coef[0:1]
            a1 = sum_rows(du) / HD
            a2 = sum_rows(du * xh) / HD
            a3 = sum_rows(du * gain2) / HD - a1 * coef[2:3] - a2 * coef[3:4]
            a4 = sum_rows(du * both) / HD - a1 * coef[4:5] - a2 * coef[5:6]
            return diag * du - coef[1:2] * (gain2 * a1 + wide * a2 + a3 + xh * a4)

        first = -(base_ref[slot(chunk)] + dot_nt(dz_after, cross))
        y = first
        dz = pull(y)
        for _ in range(STEPS - 1):
            y = first - dot_nt(dz.astype(BF16), matrix)
            dz = pull(y)
        y_ref[slot(chunk)] = y
        rounded = dz.astype(BF16)
        dz_ref[slot(chunk)] = rounded
        return rounded

    def into_state(chunk, rows, values):
        docs_row, entry = places.row_documents(chunk), places.entry(chunk)
        live, dead = docs_row == entry, docs_row != entry
        heads = head_ref[...].astype(BF16)
        given = dot_nn(
            values,
            jnp.concatenate(
                [
                    masked(rows, live),
                    masked(heads, live),
                    masked(rows, dead),
                    masked(heads, dead),
                ],
                axis=1,
            ),
        )
        dw_ref[...] += given[:, 2 * LANES : 3 * LANES]
        dc_ref[...] += given[:, 3 * LANES :]
        return given[:, :LANES], given[:, LANES : 2 * LANES]

    def reach_back(source, lam_w, lam_c):
        kept_row = places.row_documents(source) == places.last(source)
        kept_lane = places.lane_documents(source) == places.last(source)
        keys = masked(split_heads(columns(source, 1)), kept_row)
        return dot_nt(lam_w.astype(BF16), keys) + jnp.where(kept_lane, lam_c, 0.0)

    def finish(chunk):
        gain = gain_ref[...]
        query_rows = split_heads(columns(chunk, 0))
        key_rows = split_heads(columns(chunk, 1))
        entry = places.entry(chunk)
        docs_row, docs_lane = places.row_documents(chunk), places.lane_documents(chunk)
        live, dead = docs_lane == entry, docs_lane != entry
        kept = docs_lane == places.last(chunk)
        same_doc = docs_row == docs_lane
        y = y_ref[slot(chunk)]
        g = g_ref[chunk]
        coef = coef_ref[slot(chunk)]
        dz = dz_ref[slot(chunk)]
        dout = dout_ref[slot(chunk)]
        xh = norm_ref[slot(chunk)]
        rate = rate_ref[chunk]
        logits = (sum_rows(g * y) * rate * (1.0 - HD * MB * rate)).astype(BF16)
        dbias_ref[...] += logits.astype(F32)
        rated = (g * rate).astype(BF16)
        du = y * coef[0:1]
        dg = du - sum_rows(du) / HD - xh * (sum_rows(du * xh) / HD)
        tied = dg * gain
        dgain_ref[...] += dg * (2.0 * gain * xh + target_ref[chunk])
        dshift_ref[...] += tied
        tied = tied.astype(BF16)
        earlier = earlier_ref[...]
        later = earlier_ref[...].T
        t_out = masked(dot_tn(rated, dout) * output_ref[...], same_doc).astype(BF16)
        t_in = masked(
            dot_tn(rated, dz) * earlier + dot_tn(dz, rated) * later, same_doc
        ).astype(BF16)
        states = jnp.concatenate([state_ref[chunk], w_ref[...]], axis=0).astype(BF16)
        dq = dot_tn(jnp.concatenate([masked(dout, live), masked(dout, dead)], axis=0), states)
        dq = dq - dot_tn(t_out, key_rows)
        sources = jnp.concatenate(
            [masked(dz, live), masked(dz, dead), masked(-rated, kept), tied], axis=0
        )
        pick = selector()
        dk = dot_tn(
            sources, jnp.concatenate([states, lam_ref[slot(chunk)].astype(BF16), pick], axis=0)
        )
        dk = dk - dot_nn(
            jnp.concatenate([t_out, t_in], axis=1),
            jnp.concatenate([query_rows, key_rows], axis=0),
        )
        dv = -dot_tn(tied, pick)
        rows = chunk_rows(chunk)
        dproj_ref[rows, 0:LANES] = (join_heads(dq) + dinner_ref[rows, :].astype(F32)).astype(BF16)
        dproj_ref[rows, LANES : 2 * LANES] = join_heads(dk).astype(BF16)
        dproj_ref[rows, 2 * LANES : 3 * LANES] = join_heads(dv).astype(BF16)
        dproj_ref[rows, 3 * LANES : 4 * LANES] = dgate_ref[rows, :]
        diagonal = masked(
            jnp.broadcast_to(logits.astype(F32), (LANES, LANES)), square_iota(0) == square_iota(1)
        ).astype(BF16)
        head_column = (square_iota(1) == (square_iota(0) >> 6)).astype(F32).astype(BF16)
        spread = dot_nn(diagonal, head_column)
        dproj_ref[rows, 4 * LANES :] = (spread[:CHUNK] + spread[CHUNK:]).astype(BF16)

    last = chunks - 1
    prepare(last)
    base_ref[slot(last)] = free_ref[slot(last)]

    def body(index, carry):
        chunk = last - index
        lam_w, lam_c, dz_after = carry
        for step, when in enumerate(BACKWARD_STEPS):
            pl.when(index == when)(gather.steps[step])
        after = wrap(chunk + 1, chunks)
        cross = mx_ref[chunk + 1]
        dz = chain(chunk, dz_after, cross)
        add_w, add_c = into_state(after, split_heads(columns(after, 1)), dz_after)
        lam_w, lam_c = lam_w + add_w, lam_c + add_c
        lam_ref[slot(chunk)] = lam_w
        keep = places.keeps(chunk)
        dw_ref[...] += (1.0 - keep) * lam_w
        dc_ref[...] += (1.0 - keep) * lam_c
        add_w, add_c = into_state(chunk, split_heads(columns(chunk, 0)), dout_ref[slot(chunk)])
        lam_w, lam_c = keep * lam_w + add_w, keep * lam_c + add_c
        before = wrap(chunk - 1, chunks)

        @pl.when(chunk > 0)
        def _():
            prepare(before)
            base_ref[slot(before)] = free_ref[slot(before)] + reach_back(before, lam_w, lam_c)

        @pl.when(index > 0)
        def _():
            finish(after)

        return lam_w, lam_c, dz

    zero = jnp.zeros((HD, LANES), F32)
    lam_w, lam_c, dz = lax.fori_loop(
        0, chunks, body, (zero, zero, jnp.zeros((HD, LANES), BF16))
    )
    add_w, add_c = into_state(0, split_heads(columns(0, 1)), dz)
    dw_ref[...] += lam_w + add_w
    dc_ref[...] += lam_c + add_c
    finish(0)
    gather.end()


def whole_vmem(count):
    return [pl.BlockSpec(memory_space=pltpu.VMEM) for _ in range(count)]


def inner_forward(starts, proj, rates, ttt_w, ttt_b, gain, shift, own, number):
    tokens = proj.shape[0]
    chunks = tokens // CHUNK
    cell = jax.ShapeDtypeStruct((chunks, HD, LANES), F32)
    square = jax.ShapeDtypeStruct((HD, LANES), F32)
    return pl.pallas_call(
        forward_kernel,
        out_shape=[
            jax.ShapeDtypeStruct((tokens, LANES), BF16),
            cell,
            cell,
            cell,
            jax.ShapeDtypeStruct((chunks + 1, HD, LANES), F32),
            cell,
            jax.ShapeDtypeStruct((chunks + 1, LANES, LANES), BF16),
            jax.ShapeDtypeStruct((chunks + 1, LANES, LANES), BF16),
            jax.ShapeDtypeStruct((chunks, LANES, LANES), BF16),
            square,
            square,
            jax.ShapeDtypeStruct((RING, HD, LANES), F32),
            jax.ShapeDtypeStruct((RING, 8, LANES), F32),
            gathered_shape(own),
        ],
        in_specs=[pl.BlockSpec(memory_space=pltpu.SMEM)] + whole_vmem(6) + [ANYWHERE],
        out_specs=whole_vmem(13) + [ANYWHERE],
        scratch_shapes=[
            pltpu.VMEM((LANES, LANES), F32),
            pltpu.VMEM((LANES, LANES), F32),
            pltpu.VMEM((LANES, LANES), F32),
            pltpu.VMEM((HD, LANES), F32),
            pltpu.VMEM((HD, LANES), F32),
        ]
        + gather_scratch(),
        compiler_params=pltpu.CompilerParams(
            collective_id=number, has_side_effects=True, vmem_limit_bytes=20 * 1024 * 1024
        ),
        name="inner_forward",
    )(starts, proj, rates, ttt_w, ttt_b, gain, shift, own)


def inner_backward(starts, proj, rates, d_inner, d_gate, own, kept, number):
    tokens = proj.shape[0]
    chunks = tokens // CHUNK
    square = jax.ShapeDtypeStruct((HD, LANES), F32)
    cell = jax.ShapeDtypeStruct((RING, HD, LANES), F32)
    cell16 = jax.ShapeDtypeStruct((RING, HD, LANES), BF16)
    return pl.pallas_call(
        backward_kernel,
        out_shape=[
            jax.ShapeDtypeStruct((tokens, 5 * LANES), BF16),
            jax.ShapeDtypeStruct((1, LANES), F32),
            square,
            square,
            square,
            square,
            cell16,
            cell,
            cell,
            cell,
            cell,
            cell,
            cell,
            jax.ShapeDtypeStruct((RING, 8, LANES), F32),
            cell,
            cell16,
            cell,
            gathered_shape(own),
        ],
        in_specs=[pl.BlockSpec(memory_space=pltpu.SMEM)]
        + whole_vmem(4)
        + [ANYWHERE]
        + whole_vmem(len(kept)),
        out_specs=whole_vmem(17) + [ANYWHERE],
        scratch_shapes=[
            pltpu.VMEM((LANES, LANES), F32),
            pltpu.VMEM((LANES, LANES), F32),
            pltpu.VMEM((LANES, LANES), F32),
        ]
        + gather_scratch(),
        compiler_params=pltpu.CompilerParams(
            collective_id=number, has_side_effects=True, vmem_limit_bytes=24 * 1024 * 1024
        ),
        name="inner_backward",
    )(starts, proj, rates, d_inner, d_gate, own, *kept)


def heads_of_lanes(values):
    return jnp.sum(values.reshape(HD, 2, HD), axis=2).T


def project_kernel(x_ref, w_ref, rate_w_ref, bias_ref, proj_ref, rate_ref):
    x = x_ref[...]
    proj_ref[...] = dot_nn(x, w_ref[...]).astype(BF16)
    logits = dot_nt(rate_w_ref[...], x)
    for index in range(rate_ref.shape[0]):
        tokens = slice(index * CHUNK, (index + 1) * CHUNK)
        lanes = jnp.concatenate([logits[0:1, tokens], logits[1:2, tokens]], axis=1)
        rate_ref[index] = jax.nn.sigmoid(lanes + bias_ref[...]) / (HD * MB)


def project(gathered, w_in, w_rate, rate_bias):
    tokens, width = gathered.shape
    columns = w_in.shape[1]
    block = 4 * CHUNK
    rate_w = jnp.pad(w_rate.T, ((0, 14), (0, 0)))
    bias = jnp.repeat(rate_bias, HD)[None]
    return pl.pallas_call(
        project_kernel,
        grid=(tokens // block,),
        out_shape=[
            jax.ShapeDtypeStruct((tokens, columns), BF16),
            jax.ShapeDtypeStruct((tokens // CHUNK, 1, LANES), F32),
        ],
        in_specs=[
            pl.BlockSpec((block, width), lambda i: (i, 0)),
            pl.BlockSpec((width, columns), lambda i: (0, 0)),
            pl.BlockSpec((16, width), lambda i: (0, 0)),
            pl.BlockSpec((1, LANES), lambda i: (0, 0)),
        ],
        out_specs=[
            pl.BlockSpec((block, columns), lambda i: (i, 0)),
            pl.BlockSpec((block // CHUNK, 1, LANES), lambda i: (i, 0, 0)),
        ],
        compiler_params=pltpu.CompilerParams(vmem_limit_bytes=12 * 1024 * 1024),
        name="project",
    )(gathered, w_in, rate_w, bias)


def mean_columns(values):
    return jnp.mean(values, axis=1, keepdims=True)


GELU_RATE = 0.7978845608028654
GELU_CUBE = 0.044715


def gelu_parts(x):
    square = x * x
    tanh = jnp.tanh(GELU_RATE * x * (1.0 + GELU_CUBE * square))
    half = 0.5 * (1.0 + tanh)
    slope = half + 0.5 * x * (1.0 - tanh * tanh) * GELU_RATE * (1.0 + 3.0 * GELU_CUBE * square)
    return x * half, slope


def line_of(gains_ref, index):
    return jnp.concatenate(
        [gains_ref[k, index : index + 1, :] for k in range(gains_ref.shape[0])], axis=1
    )


def post_norm_of(inner_ref):
    inner = inner_ref[...].astype(F32)
    centred = inner - mean_columns(inner)
    rstd = lax.rsqrt(mean_columns(centred * centred) + EPS)
    return centred * rstd, rstd


def middle_forward_kernel(
    inner_ref, gate_ref, gains_ref, tokens_ref, ffn_gain_ref, w_ref, mixed_ref, hidden_ref, norm_ref
):
    xp, _ = post_norm_of(inner_ref)
    post = xp * line_of(gains_ref, 0) + line_of(gains_ref, 1)
    act, _ = gelu_parts(gate_ref[...].astype(F32))
    mixed = (post * act).astype(BF16)
    mixed_ref[...] = mixed
    pieces, _, piece = w_ref.shape
    for k in range(pieces):
        columns = slice(k * piece, (k + 1) * piece)
        hidden_ref[:, columns] = tokens_ref[:, columns].astype(F32) + dot_nn(mixed, w_ref[k])
    hidden = hidden_ref[...]
    scale = lax.rsqrt(mean_columns(hidden * hidden) + EPS)
    norm_ref[...] = (hidden * scale * ffn_gain_ref[...]).astype(BF16)


def middle_forward(inner, gate, gains, tokens, ffn_gain, w_out):
    shape = tokens.shape
    return pl.pallas_call(
        middle_forward_kernel,
        out_shape=[
            jax.ShapeDtypeStruct(shape, BF16),
            jax.ShapeDtypeStruct(shape, F32),
            jax.ShapeDtypeStruct(shape, BF16),
        ],
        in_specs=whole_vmem(6),
        out_specs=whole_vmem(3),
        compiler_params=pltpu.CompilerParams(vmem_limit_bytes=24 * 1024 * 1024),
        name="middle_forward",
    )(inner, gate, gains, tokens, ffn_gain, w_out)


def middle_backward_kernel(
    d_norm_ref,
    hidden_ref,
    cot_ref,
    ffn_gain_ref,
    inner_ref,
    gate_ref,
    gains_ref,
    w_ref,
    d_res_ref,
    d_mix_ref,
    d_inner_ref,
    d_gate_ref,
    sums_ref,
):
    hidden = hidden_ref[...]
    scale = lax.rsqrt(mean_columns(hidden * hidden) + EPS)
    d_norm = d_norm_ref[...]
    weighted = d_norm * ffn_gain_ref[...]
    normed = hidden * scale
    d_res = cot_ref[...].astype(F32) + scale * (
        weighted - normed * mean_columns(weighted * normed)
    )
    d_res_ref[...] = d_res
    d_mix_ref[...] = d_res.astype(BF16)
    pieces, _, piece = w_ref.shape
    d_mixed = dot_nt(d_mix_ref[:, 0:piece], w_ref[0])
    for k in range(1, pieces):
        d_mixed = d_mixed + dot_nt(d_mix_ref[:, k * piece : (k + 1) * piece], w_ref[k])
    xp, rstd = post_norm_of(inner_ref)
    post_gain = line_of(gains_ref, 0)
    post = xp * post_gain + line_of(gains_ref, 1)
    act, slope = gelu_parts(gate_ref[...].astype(F32))
    d_post = d_mixed * act
    d_gate_ref[...] = (d_mixed * post * slope).astype(BF16)
    dx = d_post * post_gain
    d_inner = rstd * (dx - mean_columns(dx) - xp * mean_columns(dx * xp))
    d_inner_ref[...] = d_inner.astype(BF16)
    lines = (sum_rows(d_post * xp), sum_rows(d_post), sum_rows(d_norm * normed))
    for k in range(sums_ref.shape[0]):
        columns = slice(k * LANES, (k + 1) * LANES)
        sums_ref[k] = jnp.concatenate(
            [line[:, columns] for line in lines] + [jnp.zeros((5, LANES), F32)], axis=0
        )


def middle_backward(d_norm, hidden, cotangent, ffn_gain, inner, gate, gains, w_out):
    shape = cotangent.shape
    return pl.pallas_call(
        middle_backward_kernel,
        out_shape=[
            jax.ShapeDtypeStruct(shape, F32),
            jax.ShapeDtypeStruct(shape, BF16),
            jax.ShapeDtypeStruct(shape, BF16),
            jax.ShapeDtypeStruct(shape, BF16),
            jax.ShapeDtypeStruct(gains.shape, F32),
        ],
        in_specs=whole_vmem(8),
        out_specs=whole_vmem(5),
        compiler_params=pltpu.CompilerParams(vmem_limit_bytes=32 * 1024 * 1024),
        name="middle_backward",
    )(d_norm, hidden, cotangent, ffn_gain, inner, gate, gains, w_out)


RING_X = 4
RING_Y = 4
GROUP = RING_X * RING_Y
UNITS = 4
MESH = pl.DeviceIdType.MESH


def place_at(head, dx, dy):
    return lax.rem(head // RING_Y + dx + RING_X, RING_X) * RING_Y + lax.rem(
        lax.rem(head, RING_Y) + dy + RING_Y, RING_Y
    )


def neighbours(head):
    return {
        (axis, way): place_at(head, way if axis == 0 else 0, way if axis == 1 else 0)
        for axis in (0, 1)
        for way in (1, -1)
    }


def greet(peers):
    barrier = pltpu.get_barrier_semaphore()
    for peer in peers:
        pl.semaphore_signal(barrier, inc=1, device_id=peer, device_id_type=MESH)
    pl.semaphore_wait(barrier, len(peers))


def moved(place, axis, way):
    shift = (way, 0) if axis == 0 else (0, way)
    return tuple((p - s) % n for p, s, n in zip(place, shift, (RING_X, RING_Y)))


class Gather:
    def __init__(self, own_ref, full_ref, send_sem, recv_sem, local_sem):
        self.own_ref, self.full_ref = own_ref, full_ref
        self.send_sem, self.recv_sem, self.local_sem = send_sem, recv_sem, local_sem
        self.head = lax.axis_index("head")
        self.near = neighbours(self.head)
        self.rows = own_ref.shape[0]
        self.unit_rows = self.rows // UNITS
        self.count = 0
        self.halves = ((0, (0, 1)), (1, (2, 3)))
        self.steps = [
            partial(self.first_arrivals, 0),
            partial(self.first_arrivals, 1),
            partial(self.second_hops, (0,)),
            self.far_arrivals,
            partial(self.second_hops, (1,)),
            partial(self.second_hops, (3,)),
            partial(self.second_hops, (2,)),
        ]

    def slab(self, place, unit):
        start = place_at(self.head, *place) * self.rows + unit * self.unit_rows
        return self.full_ref.at[pl.ds(pl.multiple_of(start, self.unit_rows), self.unit_rows)]

    def arrival(self, place, unit):
        return self.recv_sem.at[(place[0] * RING_Y + place[1]) * UNITS + unit]

    def send(self, place, unit, axis, way):
        source = (
            self.own_ref.at[pl.ds(unit * self.unit_rows, self.unit_rows)]
            if place == (0, 0)
            else self.slab(place, unit)
        )
        pltpu.make_async_remote_copy(
            src_ref=source,
            dst_ref=self.slab(place, unit),
            send_sem=self.send_sem.at[self.count],
            recv_sem=self.arrival(moved(place, axis, way), unit),
            device_id={"head": self.near[axis, way]},
            device_id_type=MESH,
        ).start()
        self.count += 1

    def waiter(self, place, unit, send_number=0):
        return pltpu.make_async_remote_copy(
            src_ref=self.slab(place, unit),
            dst_ref=self.slab(place, unit),
            send_sem=self.send_sem.at[send_number],
            recv_sem=self.arrival(place, unit),
            device_id={"head": self.near[0, 1]},
            device_id_type=MESH,
        )

    def arrive(self, place, unit):
        self.waiter(place, unit).wait_recv()

    def own_copy(self):
        start = pl.multiple_of(self.head * self.rows, self.rows)
        return pltpu.make_async_copy(
            self.own_ref, self.full_ref.at[pl.ds(start, self.rows)], self.local_sem
        )

    def cross(self, axis, first, second):
        first, second = first % RING_X, second % RING_X
        return (first, second) if axis == 0 else (second, first)

    def start(self):
        greet([{"head": peer} for peer in self.near.values()])
        self.own_copy().start()
        for turned in (False, True):
            for axis, units in self.halves:
                for unit in units:
                    for way in (1, -1):
                        self.send((0, 0), unit, 1 - axis if turned else axis, way)

    def first_arrivals(self, step):
        for axis, units in self.halves:
            for way in (1, -1):
                place = self.cross(axis, -way, 0)
                unit = units[0 if (way == 1) == (step == 0) else 1]
                self.arrive(place, unit)
                if step == 0:
                    self.send(place, unit, axis, way)
                for turn in (1, -1):
                    self.send(place, unit, 1 - axis, turn)

    def second_hops(self, firsts):
        for first in firsts:
            for axis, units in self.halves:
                for way in (1, -1):
                    unit = units[0 if way == 1 else 1]
                    place = self.cross(axis, first, -way)
                    self.arrive(place, unit)
                    self.send(place, unit, 1 - axis, way)

    def far_arrivals(self):
        for way in (1, -1):
            for axis, units in self.halves:
                unit = units[0 if way == 1 else 1]
                place = self.cross(axis, 2, 0)
                self.arrive(place, unit)
                for turn in (1, -1):
                    self.send(place, unit, 1 - axis, turn)

    def end(self):
        for first in range(RING_X):
            for axis, units in self.halves:
                for way in (1, -1):
                    self.arrive(self.cross(axis, first, -way), units[1 if way == 1 else 0])
        for first in range(RING_X):
            for axis, units in self.halves:
                for unit in units:
                    self.arrive(self.cross(axis, first, 2), unit)
        for number in range(TRANSFERS):
            self.waiter((0, 0), 0, number).wait_send()
        self.own_copy().wait()


TRANSFERS = UNITS * (GROUP - 1)
STAGED = 32
ANYWHERE = pl.BlockSpec(memory_space=pl.ANY)


def gather_kernel(*refs):
    gather = Gather(*refs)
    gather.start()
    for step in gather.steps:
        step()
    gather.end()


def gather_scratch():
    return [
        pltpu.SemaphoreType.DMA((TRANSFERS,)),
        pltpu.SemaphoreType.DMA((UNITS * GROUP,)),
        pltpu.SemaphoreType.DMA,
    ]


def gathered_shape(own):
    return jax.ShapeDtypeStruct((own.shape[0] * GROUP, own.shape[1]), own.dtype)


def gather_rows(own, number):
    return pl.pallas_call(
        gather_kernel,
        out_shape=gathered_shape(own),
        in_specs=[ANYWHERE],
        out_specs=ANYWHERE,
        scratch_shapes=gather_scratch(),
        compiler_params=pltpu.CompilerParams(collective_id=number, has_side_effects=True),
        name="gather_rows",
    )(own)


class SmallSums:
    def __init__(self, shard_ref, shard_out, lines_out, held, send_sem, recv_sem, *line_sems):
        self.shard_ref, self.shard_out, self.lines_out = shard_ref, shard_out, lines_out
        self.held, self.send_sem, self.recv_sem = held, send_sem, recv_sem
        self.line_send, self.line_recv = line_sems
        head, seq = lax.axis_index("head"), lax.axis_index("seq")
        self.head = head
        self.seqs = held.shape[0]
        self.seq_peers = [lax.rem(seq + ahead, self.seqs) for ahead in range(1, self.seqs)]
        self.head_peers = [lax.rem(head + ahead, GROUP) for ahead in range(1, GROUP)]

    def peers(self):
        return [{"seq": peer} for peer in self.seq_peers] + [
            {"head": peer} for peer in self.head_peers
        ]

    def start(self):
        self.sends = []
        for ahead, peer in enumerate(self.seq_peers, 1):
            done = pltpu.make_async_remote_copy(
                src_ref=self.shard_ref,
                dst_ref=self.held.at[ahead],
                send_sem=self.send_sem.at[ahead],
                recv_sem=self.recv_sem.at[ahead],
                device_id={"seq": peer},
                device_id_type=MESH,
            )
            done.start()
            self.sends.append(done)

    def turn(self):
        for done in self.sends:
            done.wait_recv()
        shard = self.shard_ref[...]
        for ahead in range(1, self.seqs):
            shard = shard + self.held[ahead]
        self.shard_out[...] = shard
        self.lines_out[self.head] = shard[0:8]
        self.passed = []
        for ahead, peer in enumerate(self.head_peers, 1):
            done = pltpu.make_async_remote_copy(
                src_ref=self.shard_out.at[0:8],
                dst_ref=self.lines_out.at[self.head],
                send_sem=self.line_send.at[ahead],
                recv_sem=self.line_recv.at[ahead],
                device_id={"head": peer},
                device_id_type=MESH,
            )
            done.start()
            self.passed.append(done)

    def end(self):
        for done in self.passed:
            done.wait_recv()
        for done in self.sends + self.passed:
            done.wait_send()


def everywhere_kernel(part_ref, sum_ref, seq_held, line_ref, head_held, *sems):
    head, seq = lax.axis_index("head"), lax.axis_index("seq")
    seqs = seq_held.shape[0]
    seq_peers = [lax.rem(seq + ahead, seqs) for ahead in range(1, seqs)]
    head_peers = [lax.rem(head + ahead, GROUP) for ahead in range(1, GROUP)]
    greet([{"seq": peer} for peer in seq_peers] + [{"head": peer} for peer in head_peers])

    def exchange(source, held, axis, peers, send_sem, recv_sem):
        sends = []
        for ahead, peer in enumerate(peers, 1):
            done = pltpu.make_async_remote_copy(
                src_ref=source,
                dst_ref=held.at[ahead],
                send_sem=send_sem.at[ahead],
                recv_sem=recv_sem.at[ahead],
                device_id={axis: peer},
                device_id_type=MESH,
            )
            done.start()
            sends.append(done)
        total = source[...]
        for ahead, done in enumerate(sends, 1):
            done.wait_recv()
            total = total + held[ahead]
        return total, sends

    line_ref[...], sends = exchange(part_ref, seq_held, "seq", seq_peers, *sems[:2])
    sum_ref[...], passed = exchange(line_ref, head_held, "head", head_peers, *sems[2:])
    for done in sends + passed:
        done.wait_send()


def sum_everywhere(part, seqs, number):
    return pl.pallas_call(
        everywhere_kernel,
        out_shape=jax.ShapeDtypeStruct(part.shape, F32),
        in_specs=whole_vmem(1),
        out_specs=pl.BlockSpec(memory_space=pltpu.VMEM),
        scratch_shapes=[
            pltpu.VMEM((seqs,) + part.shape, F32),
            pltpu.VMEM(part.shape, F32),
            pltpu.VMEM((GROUP,) + part.shape, F32),
            pltpu.SemaphoreType.DMA((seqs,)),
            pltpu.SemaphoreType.DMA((seqs,)),
            pltpu.SemaphoreType.DMA((GROUP,)),
            pltpu.SemaphoreType.DMA((GROUP,)),
        ],
        compiler_params=pltpu.CompilerParams(
            collective_id=number, has_side_effects=True, vmem_limit_bytes=4 * 1024 * 1024
        ),
        name="sum_everywhere",
    )(part)


def scatter_kernel(part_ref, sum_ref, held_ref, stage_ref, send_sem, recv_sem):
    scatter_body(None, part_ref, sum_ref, held_ref, stage_ref, send_sem, recv_sem)


def scatter_small_kernel(
    part_ref,
    shard_ref,
    sum_ref,
    shard_out,
    lines_out,
    held_ref,
    stage_ref,
    send_sem,
    recv_sem,
    *scratch,
):
    small = SmallSums(shard_ref, shard_out, lines_out, *scratch)
    scatter_body(small, part_ref, sum_ref, held_ref, stage_ref, send_sem, recv_sem)


def scatter_body(small, part_ref, sum_ref, held_ref, stage_ref, send_sem, recv_sem):
    head = lax.axis_index("head")
    near = neighbours(head)
    rows = sum_ref.shape[0]
    unit_rows = rows // UNITS
    peers = [{"head": peer} for peer in near.values()]
    greet(peers if small is None else small.peers())
    sends, blocks, staged = [], [], {}

    def slab(place, unit):
        start = place_at(head, *place) * rows + unit * unit_rows
        return part_ref.at[pl.ds(pl.multiple_of(start, unit_rows), unit_rows)]

    def held(index):
        return pl.ds(index * unit_rows, unit_rows)

    def stage(place, unit, total):
        block = stage_ref.at[held(len(blocks))]
        block[...] = total.astype(BF16)
        blocks.append(block)
        staged[place, unit] = block

    def send(place, unit, axis, way):
        index = len(sends)
        done = pltpu.make_async_remote_copy(
            src_ref=staged.get((place, unit), slab(place, unit)),
            dst_ref=held_ref.at[held(index)],
            send_sem=send_sem.at[index],
            recv_sem=recv_sem.at[index],
            device_id={"head": near[axis, way]},
            device_id_type=MESH,
        )
        done.start()
        sends.append(done)
        return index

    def arrived(index):
        sends[index].wait_recv()
        return held_ref[held(index)].astype(F32)

    def add_to(place, unit, *indices):
        total = staged.get((place, unit), slab(place, unit))[...].astype(F32)
        for index in indices:
            total = total + arrived(index)
        return total

    def cross(axis, first, second):
        first, second = first % RING_X, second % RING_X
        return (first, second) if axis == 0 else (second, first)

    halves = ((1, (0, 1)), (0, (2, 3)))

    def far(axis, units, other):
        return {
            way: send(cross(axis, 2, other), units[0 if way == 1 else 1], axis, way)
            for way in (1, -1)
        }

    def plain(axis, units, other):
        return {
            way: send(cross(axis, way, other), units[1 if way == 1 else 0], axis, way)
            for way in (1, -1)
        }

    def onward(axis, units, other, from_far):
        result = {}
        for way in (1, -1):
            place, unit = cross(axis, way, other), units[0 if way == 1 else 1]
            stage(place, unit, add_to(place, unit, from_far[way]))
            result[way] = send(place, unit, axis, way)
        return result

    def collect(axis, units, other, by_plain, by_onward):
        place = cross(axis, 0, other)
        return [
            add_to(place, units[0], by_onward[1], by_plain[-1]),
            add_to(place, units[1], by_onward[-1], by_plain[1]),
        ]

    order = (2, 1, 3, 0)
    fars = {(axis, o): far(axis, units, o) for o in order for axis, units in halves}
    plains = {(axis, o): plain(axis, units, o) for o in order for axis, units in halves}
    if small is not None:
        small.start()
    onwards = {
        (axis, o): onward(axis, units, o, fars[axis, o]) for o in order for axis, units in halves
    }
    last_far, last_plain, last_onward = {}, {}, {}

    def first_sum(axis, units, other):
        totals = collect(axis, units, other, plains[axis, other], onwards[axis, other])
        place = cross(axis, 0, other)
        for unit, total in zip(units, totals):
            stage(place, unit, total)

    for axis, units in halves:
        first_sum(axis, units, 2)
        last_far[axis] = far(1 - axis, units, 0)
    for axis, units in halves:
        first_sum(axis, units, 1)
        first_sum(axis, units, 3)
        last_plain[axis] = plain(1 - axis, units, 0)
    for axis, units in halves:
        last_onward[axis] = onward(1 - axis, units, 0, last_far[axis])
    if small is not None:
        small.turn()
    for axis, units in halves:
        own = collect(axis, units, 0, plains[axis, 0], onwards[axis, 0])
        extra = (
            (last_onward[axis][1], last_plain[axis][-1]),
            (last_onward[axis][-1], last_plain[axis][1]),
        )
        for unit, total, indices in zip(units, own, extra):
            for index in indices:
                total = total + arrived(index)
            sum_ref[pl.ds(unit * unit_rows, unit_rows), :] = total
    for done in sends:
        done.wait_send()
    if small is not None:
        small.end()


def scatter_scratch(rows, width):
    return [
        pltpu.VMEM((TRANSFERS * rows // UNITS, width), BF16),
        pltpu.VMEM((STAGED * rows // UNITS, width), BF16),
        pltpu.SemaphoreType.DMA((TRANSFERS,)),
        pltpu.SemaphoreType.DMA((TRANSFERS,)),
    ]


def scatter_rows(part, number):
    rows, width = part.shape[0] // GROUP, part.shape[1]
    return pl.pallas_call(
        scatter_kernel,
        out_shape=jax.ShapeDtypeStruct((rows, width), F32),
        in_specs=[pl.BlockSpec(memory_space=pltpu.VMEM)],
        out_specs=pl.BlockSpec(memory_space=pltpu.VMEM),
        scratch_shapes=scatter_scratch(rows, width),
        compiler_params=pltpu.CompilerParams(
            collective_id=number, has_side_effects=True, vmem_limit_bytes=28 * 1024 * 1024
        ),
        name="scatter_rows",
    )(part)


def scatter_rows_and_small(part, shard, seqs, number):
    rows, width = part.shape[0] // GROUP, part.shape[1]
    return pl.pallas_call(
        scatter_small_kernel,
        out_shape=[
            jax.ShapeDtypeStruct((rows, width), F32),
            jax.ShapeDtypeStruct(shard.shape, F32),
            jax.ShapeDtypeStruct((GROUP, 8, LANES), F32),
        ],
        in_specs=whole_vmem(2),
        out_specs=whole_vmem(3),
        scratch_shapes=scatter_scratch(rows, width)
        + [
            pltpu.VMEM((seqs,) + shard.shape, F32),
            pltpu.SemaphoreType.DMA((seqs,)),
            pltpu.SemaphoreType.DMA((seqs,)),
            pltpu.SemaphoreType.DMA((GROUP,)),
            pltpu.SemaphoreType.DMA((GROUP,)),
        ],
        compiler_params=pltpu.CompilerParams(
            collective_id=number, has_side_effects=True, vmem_limit_bytes=28 * 1024 * 1024
        ),
        name="scatter_rows_and_small",
    )(part, shard)


def to_tokens_kernel(
    inner_ref,
    gate_ref,
    gains_ref,
    inner_out,
    gate_out,
    gains_out,
    send_sem,
    recv_sem,
    local_sem,
):
    head = lax.axis_index("head")
    rows = inner_out.shape[0]
    first = gate_ref.shape[1] - LANES
    pairs = ((inner_ref, inner_out), (gate_ref.at[:, first:], gate_out))

    def rows_of(index):
        return pl.ds(pl.multiple_of(index * rows, rows), rows)

    def columns_of(index):
        return pl.ds(pl.multiple_of(index * LANES, LANES), LANES)

    mine = [
        pltpu.make_async_copy(
            source.at[rows_of(head)], target.at[:, columns_of(head)], local_sem.at[index]
        )
        for index, (source, target) in enumerate(pairs)
    ] + [pltpu.make_async_copy(gains_ref, gains_out.at[head], local_sem.at[2])]
    for done in mine:
        done.start()
    greet([{"head": lax.rem(head + ahead, GROUP)} for ahead in range(1, GROUP)])
    sends = []
    for ahead in range(1, GROUP):
        peer = lax.rem(head + ahead, GROUP)
        jobs = [
            (source.at[rows_of(peer)], target.at[:, columns_of(head)]) for source, target in pairs
        ] + [(gains_ref, gains_out.at[head])]
        for index, (source, target) in enumerate(jobs):
            done = pltpu.make_async_remote_copy(
                src_ref=source,
                dst_ref=target,
                send_sem=send_sem.at[ahead, index],
                recv_sem=recv_sem.at[ahead, index],
                device_id={"head": peer},
                device_id_type=MESH,
            )
            done.start()
            sends.append(done)
    for done in mine:
        done.wait()
    for done in sends:
        done.wait()


def to_tokens(inner, gate, gains, number):
    rows = inner.shape[0] // GROUP
    wide = jax.ShapeDtypeStruct((rows, GROUP * LANES), BF16)
    return pl.pallas_call(
        to_tokens_kernel,
        out_shape=[wide, wide, jax.ShapeDtypeStruct((GROUP,) + gains.shape, F32)],
        in_specs=whole_vmem(3),
        out_specs=whole_vmem(3),
        scratch_shapes=[
            pltpu.SemaphoreType.DMA((GROUP, 3)),
            pltpu.SemaphoreType.DMA((GROUP, 3)),
            pltpu.SemaphoreType.DMA((3,)),
        ],
        compiler_params=pltpu.CompilerParams(
            collective_id=number, has_side_effects=True, vmem_limit_bytes=8 * 1024 * 1024
        ),
        name="to_tokens",
    )(inner, gate, gains)


def to_heads_kernel(
    inner_ref,
    gate_ref,
    mixed_ref,
    sums_ref,
    inner_out,
    gate_out,
    mixed_out,
    sums_out,
    send_sem,
    recv_sem,
    local_sem,
):
    head = lax.axis_index("head")
    rows = inner_ref.shape[0]
    triples = ((inner_ref, inner_out), (gate_ref, gate_out), (mixed_ref, mixed_out))

    def rows_of(index):
        return pl.ds(pl.multiple_of(index * rows, rows), rows)

    def columns_of(index):
        return pl.ds(pl.multiple_of(index * LANES, LANES), LANES)

    def jobs(peer):
        return [
            (source.at[:, columns_of(peer)], target.at[rows_of(head)]) for source, target in triples
        ] + [(sums_ref.at[peer], sums_out.at[head])]

    mine = [
        pltpu.make_async_copy(source, target, local_sem.at[index])
        for index, (source, target) in enumerate(jobs(head))
    ]
    for done in mine:
        done.start()
    greet([{"head": lax.rem(head + ahead, GROUP)} for ahead in range(1, GROUP)])
    sends = []
    for ahead in range(1, GROUP):
        peer = lax.rem(head + ahead, GROUP)
        for index, (source, target) in enumerate(jobs(peer)):
            done = pltpu.make_async_remote_copy(
                src_ref=source,
                dst_ref=target,
                send_sem=send_sem.at[ahead, index],
                recv_sem=recv_sem.at[ahead, index],
                device_id={"head": peer},
                device_id_type=MESH,
            )
            done.start()
            sends.append(done)
    for done in mine:
        done.wait()
    for done in sends:
        done.wait()


def to_heads(inner, gate, mixed, sums, number):
    rows = inner.shape[0]
    tall = jax.ShapeDtypeStruct((rows * GROUP, LANES), BF16)
    return pl.pallas_call(
        to_heads_kernel,
        out_shape=[tall, tall, tall, jax.ShapeDtypeStruct(sums.shape, F32)],
        in_specs=whole_vmem(4),
        out_specs=whole_vmem(4),
        scratch_shapes=[
            pltpu.SemaphoreType.DMA((GROUP, 4)),
            pltpu.SemaphoreType.DMA((GROUP, 4)),
            pltpu.SemaphoreType.DMA((4,)),
        ],
        compiler_params=pltpu.CompilerParams(
            collective_id=number, has_side_effects=True, vmem_limit_bytes=8 * 1024 * 1024
        ),
        name="to_heads",
    )(inner, gate, mixed, sums)


def after(value, *others):
    return lax.optimization_barrier((value,) + others)[0]


def per_device(
    tokens,
    doc_starts,
    norm_gain,
    w_in,
    w_rate,
    rate_bias,
    ttt_w,
    ttt_b,
    ttt_gain,
    ttt_shift,
    post_gain,
    post_bias,
    w_out,
    ffn_gain,
    w_gate_up,
    w_down,
    cotangent,
):
    seq = lax.axis_index("seq")
    seqs = lax.axis_size("seq")
    tok_rows, width = tokens.shape
    head_count, head_dim = ttt_b.shape
    local_width = head_count * head_dim
    ffn_local = w_down.shape[0]
    w_in_flat = w_in.reshape(width, 4 * local_width)
    w_gu_flat = w_gate_up.reshape(width, 2 * ffn_local)
    ffn_gain_line = ffn_gain[None]

    piece = width // seqs
    w_out_piece = lax.dynamic_slice_in_dim(w_out, seq * piece, piece, axis=1)
    w_out_all = lax.all_gather(w_out_piece, ("seq", "head"), axis=0, tiled=True)
    w_out_all = w_out_all.reshape(seqs, width, piece)

    resid = tokens.astype(F32)
    scale_one = lax.rsqrt(jnp.mean(resid * resid, axis=-1, keepdims=True) + EPS)
    norm_one = (resid * scale_one * norm_gain).astype(BF16)
    gathered = gather_rows(norm_one, 0)
    projected, rate_lanes = project(gathered, w_in_flat, w_rate, rate_bias)
    inner, *kept, _, _, cot_rows = inner_forward(
        doc_starts, projected, rate_lanes, ttt_w, ttt_b, ttt_gain, ttt_shift, cotangent, 7
    )

    gains = jnp.concatenate(
        [post_gain[None], post_bias[None], jnp.zeros((6, local_width), F32)], axis=0
    )
    inner_tok, gate_tok, all_gains = to_tokens(inner, projected, gains, 1)
    mixed_tok, hidden_res, norm_two = middle_forward(
        inner_tok, gate_tok, all_gains, tokens, ffn_gain_line, w_out_all
    )

    ffn_rows = gather_rows(norm_two, 2)
    gate_up = dot_nn(ffn_rows, w_gu_flat).astype(BF16)
    gate_part = gate_up[:, :ffn_local].astype(F32)
    up_part = gate_up[:, ffn_local:].astype(F32)
    silu_val, silu_pull = jax.vjp(jax.nn.silu, gate_part)
    hidden_state = (silu_val * up_part).astype(BF16)
    ffn_part = dot_nn(hidden_state, w_down).astype(BF16)
    d_hidden = dot_nt(cot_rows, w_down)
    d_gate_part = silu_pull(d_hidden * up_part)[0]
    d_gate_up = jnp.concatenate([d_gate_part, d_hidden * silu_val], axis=1).astype(BF16)
    grad_w_down = dot_tn(hidden_state, cot_rows).astype(BF16)
    grad_w_gate_up = dot_tn(ffn_rows, d_gate_up).reshape(width, 2, ffn_local).astype(BF16)
    d_norm_part = dot_nt(d_gate_up, w_gu_flat).astype(BF16)
    d_norm_two = scatter_rows(after(d_norm_part, grad_w_down, grad_w_gate_up, ffn_part), 3)
    ffn_out = lax.psum_scatter(
        after(ffn_part, d_norm_two), "head", scatter_dimension=0, tiled=True
    )

    d_res, d_mix, d_inner_tok, d_gate_tok, token_sums = middle_backward(
        d_norm_two,
        hidden_res,
        cotangent,
        ffn_gain_line,
        inner_tok,
        gate_tok,
        all_gains,
        w_out_all,
    )
    d_inner, d_gate, mixed_in, head_sums = to_heads(
        d_inner_tok, d_gate_tok, mixed_tok, token_sums, 4
    )
    head_sums = jnp.sum(head_sums, axis=0)
    output = (hidden_res + ffn_out.astype(F32)).astype(BF16)

    d_projected, d_bias, d_start_w, d_start_c, d_gain, d_shift, *_, mix_rows = inner_backward(
        doc_starts, projected, rate_lanes, d_inner, d_gate, d_mix, kept, 8
    )
    grad_in = dot_tn(gathered, d_projected)
    w_columns = jnp.pad(w_rate, ((0, 0), (0, local_width - head_count)))
    w_columns = jnp.concatenate([w_in_flat, w_columns], axis=1)
    grad_w_rate = grad_in[:, 4 * local_width : 4 * local_width + head_count]
    grad_w_in = grad_in[:, : 4 * local_width].astype(BF16).reshape(width, 4, local_width)
    grad_w_out = dot_tn(mixed_in, mix_rows).astype(BF16)
    sum_w_in, sum_w_out, sum_w_down, sum_w_gate_up = lax.psum(
        after((grad_w_in, grad_w_out, grad_w_down, grad_w_gate_up), ffn_out), "seq"
    )
    singles = jnp.stack(
        [
            head_sums[2],
            head_sums[0],
            head_sums[1],
            d_start_c[:, ::head_dim].T.reshape(LANES),
            heads_of_lanes(d_gain).reshape(LANES),
            heads_of_lanes(d_shift).reshape(LANES),
            d_bias[0],
            jnp.zeros((LANES,), F32),
        ]
    )
    rate_rows = grad_w_rate.T.reshape(2 * width // LANES, LANES)
    shard = jnp.concatenate([singles, d_start_w, rate_rows], axis=0)
    d_norm_part = dot_nt(d_projected, w_columns).astype(BF16)
    d_norm_one, shard, lines = scatter_rows_and_small(
        after(d_norm_part, grad_w_in, grad_w_out), shard, seqs, 5
    )
    weighted = d_norm_one * norm_gain
    normed = resid * scale_one
    grad_tokens = d_res + scale_one * (
        weighted - normed * jnp.mean(weighted * normed, axis=-1, keepdims=True)
    )

    grad_norm_gain = jnp.sum(d_norm_one * normed, axis=0).reshape(GROUP, LANES)
    sum_norm_gain = sum_everywhere(grad_norm_gain, seqs, 6).reshape(width)
    sum_ffn_gain = lines[:, 0].reshape(width)
    sum_ttt_w = shard[8 : 8 + head_dim].reshape(head_dim, head_count, head_dim)
    per_head = (head_count, head_dim)
    return (
        output,
        grad_tokens,
        sum_norm_gain,
        sum_w_in.astype(F32),
        shard[8 + head_dim :].reshape(head_count, width).T,
        jnp.sum(shard[6].reshape(per_head), axis=1),
        sum_ttt_w.transpose(1, 2, 0),
        shard[3].reshape(per_head),
        shard[4].reshape(per_head),
        shard[5].reshape(per_head),
        shard[1],
        shard[2],
        sum_w_out.astype(F32),
        sum_ffn_gain,
        sum_w_gate_up.astype(F32),
        sum_w_down.astype(F32),
    )


def solution(mesh):
    return jax.shard_map(
        per_device,
        mesh=mesh,
        in_specs=(
            P(("seq", "head"), None),
            P("seq", None),
            P(),
            P(None, None, "head"),
            P(None, "head"),
            P("head"),
            P("head", None, None),
            P("head", None),
            P("head", None),
            P("head", None),
            P("head"),
            P("head"),
            P("head", None),
            P(),
            P(None, None, "head"),
            P("head", None),
            P(("seq", "head"), None),
        ),
        out_specs=(
            P(("seq", "head"), None),
            P(("seq", "head"), None),
            P(),
            P(None, None, "head"),
            P(None, "head"),
            P("head"),
            P("head", None, None),
            P("head", None),
            P("head", None),
            P("head", None),
            P("head"),
            P("head"),
            P("head", None),
            P(),
            P(None, None, "head"),
            P("head", None),
        ),
        check_vma=False,
    )
```

profile of v0, /device:TPU:1, one launch (start us, length us, event | category | flops | bytes accessed | tf_op | source)
XLA Modules:
  0.0 572.6 jit_solution(13341618330261254272)
XLA Ops:
  9.8 3.3 copy.46
  14.2 53.4 %gather_rows.2.x_ref = bf16[2048,2048]{1,0:T(8,128)(2,1)} custom-call(bf16[128,2048]{1,0:T(8,128)(2,1)} %fusion.18.refs_0_), custom_call_target="tpu_custom_call" | custom-call | tf_op jit(solution)/shard_map/gather_rows/pallas_call | solution.py:982
  67.8 3.4 copy-done.2
  72.8 8.0 %project.1 = (bf16[2048,512]{1,0:T(8,128)(2,1)S(1)}, f32[32,1,128]{2,1,0:T(1,128)S(1)}) custom-call(bf16[2048,2048]{1,0:T(8,128)(2,1)S(1)} %copy-done.2, bf16[2048,512]{1,0:T(8,128)(2,1)S(1)} %bitcast.47, bf16[16,2048]{1,0:T(8,128)(2,1)S(1)} %pad.8.rate_w_ref, f32[1,128]{1,0:T(1,128)S(1)} %broadcast_in_dim_reshape.3.bias_ref), custom_call_target="tpu_custom_call" | custom-call | tf_op jit(solution)/shard_map/project/pallas_call | solution.py:657
  80.9 47.3 %inner_forward.1 = (bf16[2048,128]{1,0:T(8,128)(2,1)S(1)}, f32[32,64,128]{2,1,0:T(8,128)S(1)}, f32[32,64,128]{2,1,0:T(8,128)S(1)}, f32[32,64,128]{2,1,0:T(8,128)...) custom-call(s32[1,3]{1,0:T(1,128)S(1)} %copy-done.43, ...), custom_call_target="tpu_custom_call" | custom-call | tf_op jit(solution)/shard_map/inner_forward/pallas_call | solution.py:556
  136.2 3.2 copy-done.47
  139.4 15.4 %to_tokens.1 = (bf16[128,2048]{1,0:T(8,128)(2,1)S(1)}, bf16[128,2048]{1,0:T(8,128)(2,1)S(1)}, f32[16,8,128]{2,1,0:T(8,128)S(1)}) custom-call(bf16[2048,128]{1,0:T(8,128)(2,1)S(1)} %get-tuple-element.64.inner_ref, bf16[2048,512]{1,0:T(8,128)(2,1)S(1)} %get-tuple-element.62.proj_ref.gate_ref, f32[8,128]{1,0:T(8,128)S(1)} %maximum_maximum_fusion.gains_ref), custom_call_target="tpu_custom_call" | custom-call | tf_op jit(solution)/shard_map/to_tokens/pallas_call | solution.py:1354
  156.4 3.4 copy-done.3
  166.4 48.5 %gather_rows.3 = bf16[2048,2048]{1,0:T(8,128)(2,1)} custom-call(bf16[128,2048]{1,0:T(8,128)(2,1)} %copy-done.40), custom_call_target="tpu_custom_call" | custom-call | tf_op jit(solution)/shard_map/gather_rows/pallas_call | solution.py:982
  215.0 8.6 %convolution_convert_fusion.4 = bf16[2048,688]{0,1:T(8,128)(2,1)S(1)} fusion(bf16[2048,2048]{1,0:T(8,128)(2,1)} %gather_rows.3, bf16[2048,688]{0,1:T(8,128)(2,1)S(1)} %bitcast.41), kind=kOutput, calls=%fused_computation.13 | convolution fusion | flops 5772771328 | bytes 14024704 | tf_op jit(solution)/shard_map/dot_general | solution.py:21
  223.6 7.9 %convolution_convert_fusion.5 = bf16[344,2048]{1,0:T(8,128)(2,1)} fusion(bf16[2048,2048]{1,0:T(8,128)(2,1)} %copy-done.47, bf16[2048,688]{0,1:T(8,128)(2,1)S(1)} %convolution_convert_fusion.4), kind=kOutput, calls=%fused_computation.23 | convolution fusion | flops 2892021760 | bytes 12615680 | tf_op jit(solution)/shard_map/dot_general | solution.py:29
  231.6 6.1 %fusion.7 = (bf16[2048,344]{0,1:T(8,128)(2,1)}, bf16[2048,344]{0,1:T(8,128)(2,1)}) fusion(bf16[2048,688]{0,1:T(8,128)(2,1)S(1)} %convolution_convert_fusion.4, bf16[2048,2048]{1,0:T(8,128)(2,1)S(1)} %bitcast.54, bf16[344,2048]{1,0:T(8,128)(2,1)S(1)} %copy-done.57), kind=kOutput, calls=%fused_computation.20 | convolution fusion | flops 2896953344 | bytes 15433728 | tf_op jit(solution)/shard_map/dot_general | solution.py:25
  237.7 7.0 %convolution_convert_fusion.2 = bf16[2048,2048]{1,0:T(8,128)(2,1)} fusion(bf16[344,2048]{1,0:T(8,128)(2,1)S(1)} %copy-done.57, bf16[2048,688]{0,1:T(8,128)(2,1)S(1)} %convolution_convert_fusion.4), kind=kOutput, calls=%fused_computation.2 | convolution fusion | flops 2895511552 | bytes 12615680 | tf_op jit(solution)/shard_map/dot_general | solution.py:21
  244.7 10.4 %convolution_convert_fusion.3 = bf16[2048,688]{0,1:T(8,128)(2,1)} fusion(bf16[2048,2048]{1,0:T(8,128)(2,1)} %gather_rows.3, bf16[2048,344]{0,1:T(8,128)(2,1)} %get-tuple-element.119, bf16[2048,344]{0,1:T(8,128)(2,1)} %get-tuple-element.118), kind=kOutput, calls=%fused_computation.12 | convolution fusion | flops 5778407424 | bytes 14024704 | tf_op jit(solution)/shard_map/dot_general | solution.py:29
  255.1 7.2 %convolution_convert_fusion.part_ref = bf16[2048,2048]{1,0:T(8,128)(2,1)S(1)} fusion(bf16[2048,688]{0,1:T(8,128)(2,1)S(1)} %bitcast.42, bf16[2048,344]{0,1:T(8,128)(2,1)S(1)} %copy-done.59, bf16[2048,344]{0,1:T(8,128)(2,1)S(1)} %copy-done.58), kind=kOutput, calls=%fused_computation | convolution fusion | flops 5781192704 | bytes 14024704 | tf_op jit(solution)/shard_map/dot_general | solution.py:25
  262.4 44.3 %scatter_rows.1.d_norm_ref = f32[128,2048]{1,0:T(8,128)S(1)} custom-call(bf16[2048,2048]{1,0:T(8,128)(2,1)S(1)} %convolution_convert_fusion.part_ref), custom_call_target="tpu_custom_call" | custom-call | tf_op jit(solution)/shard_map/scatter_rows/pallas_call | solution.py:1258
  308.2 3.4 copy-done.4
  313.7 4.4 middle_backward.1
  318.2 27.3 %to_heads.1 = (bf16[2048,128]{1,0:T(8,128)(2,1)S(1)}, bf16[2048,128]{1,0:T(8,128)(2,1)S(1)}, bf16[2048,128]{1,0:T(8,128)(2,1)S(1)}, f32[16,8,128]{2,1,0:T(8,128)S(1)}) custom-call(bf16[128,2048]{1,0:T(8,128)(2,1)S(1)} %get-tuple-element.74.inner_ref, bf16[128,2048]{1,0:T(8,128)(2,1)S(1)} %get-tuple-element.75.gate_ref, bf16[128,2048]{1,0:T(8,128)(2,1)S(1)} %copy-done.39, ...), custom_call_target="tpu_custom_call" | custom-call | tf_op jit(solution)/shard_map/to_heads/pallas_call | solution.py:1429
  351.7 80.8 %inner_backward.1 = (bf16[2048,640]{1,0:T(8,128)(2,1)S(1)}, f32[1,128]{1,0:T(1,128)S(1)}, f32[64,128]{1,0:T(8,128)S(1)}, f32[64,128]{1,0:T(8,128)S(1)}, f32[64,1...) custom-call(s32[1,3]{1,0:T(1,128)S(1)} %copy-done.43, ...), custom_call_target="tpu_custom_call" | custom-call | tf_op jit(solution)/shard_map/inner_backward/pallas_call | solution.py:597
  432.6 5.9 %fusion.32 = f32[2048,640]{0,1:T(8,128)S(1)} fusion(bf16[2048,2048]{1,0:T(8,128)(2,1)S(1)} %bitcast.44, bf16[2048,640]{1,0:T(8,128)(2,1)S(1)} %get-tuple-element.91), kind=kOutput, calls=%fused_computation.61 | convolution fusion | flops 5368709120 | bytes 16252928 | tf_op jit(solution)/shard_map/dot_general | solution.py:29
  440.5 2.1 convolution_convert_fusion.6
  442.6 9.3 %convolution_convert_fusion.1.part_ref = bf16[2048,2048]{1,0:T(8,128)(2,1)} fusion(bf16[2048,640]{1,0:T(8,128)(2,1)S(1)} %get-tuple-element.91, bf16[2048,2]{1,0:T(8,128)(2,1)S(1)} %copy-done.51, bf16[2048,512]{1,0:T(8,128)(2,1)S(1)} %bitcast.48), kind=kOutput, calls=%fused_computation.1 | convolution fusion | flops 5380767744 | bytes 13115392 | tf_op jit(solution)/shard_map/dot_general | solution.py:25
  452.0 4.2 copy.41
  458.3 3.4 copy-done.8
  461.6 55.4 %scatter_rows_and_small.1 = (f32[128,2048]{1,0:T(8,128)S(1)}, f32[104,128]{1,0:T(8,128)S(1)}, f32[16,8,128]{2,1,0:T(8,128)S(1)}) custom-call(bf16[2048,2048]{1,0:T(8,128)(2,1)S(1)} %copy-done.8, f32[104,128]{1,0:T(8,128)S(1)} %concatenate.16.shard_ref), custom_call_target="tpu_custom_call" | custom-call | tf_op jit(solution)/shard_map/scatter_rows_and_small/pallas_call | solution.py:1273
  521.3 13.3 %sum_everywhere.1 = f32[16,128]{1,0:T(8,128)S(1)} custom-call(f32[16,128]{1,0:T(8,128)S(1)} %bitcast.49), custom_call_target="tpu_custom_call" | custom-call | tf_op jit(solution)/shard_map/sum_everywhere/pallas_call | solution.py:1084
  535.9 2.6 fusion.22
  539.4 13.9 %all-reduce.5.cloned.1.call-done = (bf16[2048,4,128]{2,1,0:T(4,128)(2,1)}, bf16[128,2048]{1,0:T(8,128)(2,1)}, bf16[2048,2,344]{0,2,1:T(8,128)(2,1)}, bf16[344,2048]{1,0:T(8,128)(2,1)}) async-done(((bf16[2048,4,128]{2,1,0:T(4,128)(2,1)}, bf16[128,2048]{1,0:T(8,128)(2,1)}, bf16[2048,2,344]{0,2,1:T(8,128)(2,1)}, bf16[344,2048]{1,0:T(8,128)(2,1)}), (bf16[2048,4,128]{2,1,0:T(4,128)(2,1)}, ...) | async-done | bytes 6848528 | tf_op jit(solution)/shard_map/psum | solution.py:1544
  553.3 2.1 convert_element_type.79
  555.4 3.6 convert_element_type.78
  561.8 3.2 convert_element_type.80
  (180 shorter events, 45.3 us)
Async XLA Ops:
  7.2 207.8 %copy-start = (bf16[2048,2,344]{0,2,1:T(8,128)(2,1)S(1)}, bf16[2048,2,344]{0,2,1:T(8,128)(2,1)}, u32[]{:S(2)}) copy-start(bf16[2048,2,344]{0,2,1:T(8,128)(2,1)} %param.31) | copy-start | bytes 8454148
  7.2 5.9 %copy-start.7 = (bf16[128,2048]{1,0:T(8,128)(2,1)S(1)}, bf16[128,2048]{1,0:T(8,128)(2,1)}, u32[]{:S(2)}) copy-start(bf16[128,2048]{1,0:T(8,128)(2,1)} %tokens_ref.1) | copy-start | bytes 1572868
  7.2 6.0 %copy-start.53 = (f32[2048]{0:T(1024)S(1)}, f32[2048]{0:T(1024)}, u32[]{:S(2)}) copy-start(f32[2048]{0:T(1024)} %param.19) | copy-start | bytes 24580
  7.2 149.2 %all-gather.2.cloned.1.call-start = ((), (), s32[]{:S(2)}) async-start(), calls=%async_computation.1 | async-start | bytes 8454144 | tf_op jit(solution)/shard_map/all_gather | solution.py:1481
  8.9 443.0 %reduce-scatter.2.cloned.1.call-start = ((), (), s32[]{:S(2)}) async-start(), calls=%async_computation.2 | async-start | bytes 8912896 | tf_op jit(solution)/shard_map/reduce_scatter | solution.py:1515
  14.2 53.5 %copy-start.54 = (bf16[2048,2]{0,1:T(2,128)(2,1)S(1)}, bf16[2048,2]{0,1:T(2,128)(2,1)}, u32[]{:S(2)}) copy-start(bf16[2048,2]{0,1:T(2,128)(2,1)} %param.21) | copy-start | bytes 24580
  72.7 8.1 %copy-start.13 = (bf16[128,2048]{1,0:T(8,128)(2,1)S(1)}, bf16[128,2048]{1,0:T(8,128)(2,1)}, u32[]{:S(2)}) copy-start(bf16[128,2048]{1,0:T(8,128)(2,1)} %cot_ref.3) | copy-start | bytes 1572868
  72.7 8.1 %copy-start.41 = (f32[2,64,64]{2,1,0:T(8,128)S(1)}, f32[2,64,64]{2,1,0:T(8,128)}, u32[]{:S(2)}) copy-start(f32[2,64,64]{2,1,0:T(8,128)} %ttt_w_ref.1) | copy-start | bytes 98308
  72.7 8.1 %copy-start.43 = (s32[1,3]{1,0:T(1,128)S(1)}, s32[1,3]{1,0:T(1,128)}, u32[]{:S(2)}) copy-start(s32[1,3]{1,0:T(1,128)} %starts_ref.3) | copy-start | bytes 40
  72.7 8.1 %copy-start.44 = (f32[2,64]{1,0:T(2,128)S(1)}, f32[2,64]{1,0:T(2,128)}, u32[]{:S(2)}) copy-start(f32[2,64]{1,0:T(2,128)} %ttt_b_ref.1) | copy-start | bytes 1540
  72.7 8.2 %copy-start.45 = (f32[2,64]{1,0:T(2,128)S(1)}, f32[2,64]{1,0:T(2,128)}, u32[]{:S(2)}) copy-start(f32[2,64]{1,0:T(2,128)} %ttt_gain_ref.1) | copy-start | bytes 1540
  72.7 8.1 %copy-start.46 = (f32[2,64]{1,0:T(2,128)S(1)}, f32[2,64]{1,0:T(2,128)}, u32[]{:S(2)}) copy-start(f32[2,64]{1,0:T(2,128)} %ttt_shift_ref.1) | copy-start | bytes 1540
  72.8 63.4 %copy-start.55 = (f32[128]{0:T(128)S(1)}, f32[128]{0:T(128)}, u32[]{:S(2)}) copy-start(f32[128]{0:T(128)} %param.28) | copy-start | bytes 1540
  72.8 63.4 %copy-start.56 = (f32[128]{0:T(128)S(1)}, f32[128]{0:T(128)}, u32[]{:S(2)}) copy-start(f32[128]{0:T(128)} %param.27) | copy-start | bytes 1540
  80.8 58.6 %copy-start.5 = (bf16[2048,512]{1,0:T(8,128)(2,1)}, bf16[2048,512]{1,0:T(8,128)(2,1)S(1)}, u32[]{:S(2)}) copy-start(bf16[2048,512]{1,0:T(8,128)(2,1)S(1)} %get-tuple-element.62.proj_ref.gate_ref) | copy-start | bytes 6291460
  80.8 75.5 %copy-start.42 = (f32[2048]{0:T(1024)S(1)}, f32[2048]{0:T(1024)}, u32[]{:S(2)}) copy-start(f32[2048]{0:T(1024)} %param.30) | copy-start | bytes 24580
  215.0 16.5 %slice-start.2 = ((s8[8388608]{0:T(1024)(128)(4,1)}), s8[4194304]{0:T(1024)(128)(4,1)S(1)}, s32[]{:S(2)}) async-start(s8[8388608]{0:T(1024)(128)(4,1)} %bitcast.53), calls=%async_computation.6 | async-start | bytes 8388608
  223.6 7.9 %slice-start.3 = ((s8[8388608]{0:T(1024)(128)(4,1)}), s8[4194304]{0:T(1024)(128)(4,1)S(1)}, s32[]{:S(2)}) async-start(s8[8388608]{0:T(1024)(128)(4,1)} %bitcast.53), calls=%async_computation.7 | async-start | bytes 8388608
  223.6 7.9 %copy-start.57 = (bf16[344,2048]{1,0:T(8,128)(2,1)S(1)}, bf16[344,2048]{1,0:T(8,128)(2,1)}, u32[]{:S(2)}) copy-start(bf16[344,2048]{1,0:T(8,128)(2,1)} %param.32) | copy-start | bytes 4227076
  244.7 10.5 %copy-start.58 = (bf16[2048,344]{0,1:T(8,128)(2,1)S(1)}, bf16[2048,344]{0,1:T(8,128)(2,1)}, u32[]{:S(2)}) copy-start(bf16[2048,344]{0,1:T(8,128)(2,1)} %get-tuple-element.118) | copy-start | bytes 4227076
  244.7 10.5 %copy-start.59 = (bf16[2048,344]{0,1:T(8,128)(2,1)S(1)}, bf16[2048,344]{0,1:T(8,128)(2,1)}, u32[]{:S(2)}) copy-start(bf16[2048,344]{0,1:T(8,128)(2,1)} %get-tuple-element.119) | copy-start | bytes 4227076
  306.7 246.6 %all-reduce.5.cloned.1.call-start = ((), (), s32[]{:S(2)}) async-start(), calls=%async_computation.3 | async-start | bytes 13697024 | tf_op jit(solution)/shard_map/psum | solution.py:1544
  313.7 4.5 copy-start.39
  313.7 31.8 %copy-start.6 = (bf16[2048,512]{1,0:T(8,128)(2,1)S(1)}, bf16[2048,512]{1,0:T(8,128)(2,1)}, u32[]{:S(2)}) copy-start(bf16[2048,512]{1,0:T(8,128)(2,1)} %copy-done.5) | copy-start | bytes 6291460
  313.7 31.8 %copy-start.22 = (f32[33,64,128]{2,1,0:T(8,128)S(1)}, f32[33,64,128]{2,1,0:T(8,128)}, u32[]{:S(2)}) copy-start(f32[33,64,128]{2,1,0:T(8,128)} %copy-done.21) | copy-start | bytes 3244036
  313.7 31.8 %copy-start.24 = (bf16[33,128,128]{2,1,0:T(8,128)(2,1)S(1)}, bf16[33,128,128]{2,1,0:T(8,128)(2,1)}, u32[]{:S(2)}) copy-start(bf16[33,128,128]{2,1,0:T(8,128)(2,1)} %copy-done.23) | copy-start | bytes 3244036
  313.7 31.8 %copy-start.26 = (bf16[33,128,128]{2,1,0:T(8,128)(2,1)S(1)}, bf16[33,128,128]{2,1,0:T(8,128)(2,1)}, u32[]{:S(2)}) copy-start(bf16[33,128,128]{2,1,0:T(8,128)(2,1)} %copy-done.25) | copy-start | bytes 3244036
  313.7 118.8 %slice-start = ((s8[8388608]{0:T(1024)(128)(4,1)}), s8[4194304]{0:T(1024)(128)(4,1)S(1)}, s32[]{:S(2)}) async-start(s8[8388608]{0:T(1024)(128)(4,1)} %bitcast.43), calls=%async_computation.4 | async-start | bytes 8388608
  318.2 27.3 %copy-start.37 = (f32[128,2048]{1,0:T(8,128)}, f32[128,2048]{1,0:T(8,128)S(1)}, u32[]{:S(2)}) copy-start(f32[128,2048]{1,0:T(8,128)S(1)} %get-tuple-element.73) | copy-start | bytes 3145732
  318.2 114.4 %slice-start.1 = ((s8[8388608]{0:T(1024)(128)(4,1)}), s8[4194304]{0:T(1024)(128)(4,1)S(1)}, s32[]{:S(2)}) async-start(s8[8388608]{0:T(1024)(128)(4,1)} %bitcast.43), calls=%async_computation.5 | async-start | bytes 8388608
  517.1 21.4 %copy-start.52 = (bf16[128,2048]{1,0:T(8,128)(2,1)S(1)}, bf16[128,2048]{1,0:T(8,128)(2,1)}, u32[]{:S(2)}) copy-start(bf16[128,2048]{1,0:T(8,128)(2,1)} %reduce-scatter.2.cloned.1.call-done) | copy-start | bytes 1572868
  560.9 4.8 copy-start.1
  (35 other events, 58.2 us)
Sparse Core Ops, SparseCore 0:
  11.8 75.7 all-gather.1
  306.8 126.0 reduce-scatter.1
  456.3 96.8 all-reduce.4
where the time goes:
time: 583 us; the launch traced here: 573 us
  Pallas kernels  400 us (69%)
  matrix products  64.7 us (11%)
  local copies, waits for them, and re-layouts  62 us (11%)
  other arithmetic  16.9 us (3%)
  between operations  14.8 us (3%)
  waiting for transfers between devices  13.9 us (2%)
    pallas_call x2, Pallas kernels, gather_rows(): pl.pallas_call(gather_kernel, out_shape=gathered_shape(own), in_specs=[AN...  102 us
    pallas_call x1, Pallas kernels, inner_backward(): pl.pallas_call(backward_kernel, out_shape=[jax.ShapeDtypeStruct((tokens,...  80.8 us
    pallas_call x1, Pallas kernels, scatter_rows_and_small(): pl.pallas_call(scatter_small_kernel, out_shape=[jax.ShapeDtypeStruct((row...  55.4 us
    pallas_call x1, Pallas kernels, inner_forward(): pl.pallas_call(forward_kernel, out_shape=[jax.ShapeDtypeStruct((tokens, L...  47.3 us
    unnamed x131, local copies, waits for them, and re-layouts  47.1 us
    pallas_call x1, Pallas kernels, scatter_rows(): pl.pallas_call(scatter_kernel, out_shape=jax.ShapeDtypeStruct((rows, widt...  44.3 us
    pallas_call x1, Pallas kernels, to_heads(): pl.pallas_call(to_heads_kernel, out_shape=[tall, tall, tall, jax.ShapeDty...  27.3 us
    dot_general x4, matrix products, dot_tn(): lax.dot_general(a, b, (((0,), (0,)), ((), ())), preferred_element_type=F32)  26.4 us
  transfers between devices with their start and end apart: 3, of which 1 were waited for; matrix products, arithmetic and copies ran while one was open for 6% of the time, Pallas kernels for 53%

commit v1 on v0

--- a/solution.py
+++ b/solution.py
@@ -14,6 +14,7 @@
 CHUNK = STEPS * MB
 LANES = 2 * CHUNK
 BF16 = jnp.bfloat16
+MOST_VMEM = 56 * 1024 * 1024
 F32 = jnp.float32
 
 
@@ -293,6 +294,7 @@
 
 FORWARD_STEPS = (5, 7, 12, 16, 20, 24, 30)
 BACKWARD_STEPS = (5, 7, 10, 13, 17, 20, 24)
+SUM_STEPS = (6, 11, 19, 26)
 
 
 def backward_kernel(
@@ -301,6 +303,9 @@
     rate_ref,
     dinner_ref,
     dgate_ref,
+    mixed_ref,
+    grad_gu_ref,
+    grad_down_ref,
     mix_ref,
     z_ref,
     g_ref,
@@ -329,15 +334,30 @@
     y_ref,
     dz_ref,
     lam_ref,
+    mixed_out,
+    sum_gu_ref,
+    sum_down_ref,
     mix_rows_ref,
     head_ref,
     earlier_ref,
     output_ref,
-    *gather_sems,
+    send_sem,
+    recv_sem,
+    *sems,
 ):
     chunks = rate_ref.shape[0]
-    gather = Gather(mix_ref, mix_rows_ref, *gather_sems)
-    gather.start()
+    gather = Gather(mix_ref, mix_rows_ref, *sems[2 * SEQ_SUM_SCRATCH :])
+    sums = (
+        SeqSum(0, grad_gu_ref, sum_gu_ref, *sems[:SEQ_SUM_SCRATCH]),
+        SeqSum(1, grad_down_ref, sum_down_ref, *sems[SEQ_SUM_SCRATCH : 2 * SEQ_SUM_SCRATCH]),
+    )
+    exchange = ToHeads(
+        [(dgate_ref, dproj_ref, 3 * LANES), (mixed_ref, mixed_out, 0)], send_sem, recv_sem
+    )
+    gather.start([{"head": peer} for peer in exchange.peers] + sums[0].peers())
+    exchange.start()
+    for total in sums:
+        total.start()
     places = Places(starts_ref)
     inner_masks(head_ref, earlier_ref, output_ref)
     dbias_ref[...] = jnp.zeros_like(dbias_ref)
@@ -492,7 +512,6 @@
         dproj_ref[rows, 0:LANES] = (join_heads(dq) + dinner_ref[rows, :].astype(F32)).astype(BF16)
         dproj_ref[rows, LANES : 2 * LANES] = join_heads(dk).astype(BF16)
         dproj_ref[rows, 2 * LANES : 3 * LANES] = join_heads(dv).astype(BF16)
-        dproj_ref[rows, 3 * LANES : 4 * LANES] = dgate_ref[rows, :]
         diagonal = masked(
             jnp.broadcast_to(logits.astype(F32), (LANES, LANES)), square_iota(0) == square_iota(1)
         ).astype(BF16)
@@ -509,6 +528,9 @@
         lam_w, lam_c, dz_after = carry
         for step, when in enumerate(BACKWARD_STEPS):
             pl.when(index == when)(gather.steps[step])
+        for step, when in enumerate(SUM_STEPS):
+            for total in sums:
+                pl.when(index == when)(total.steps[step])
         after = wrap(chunk + 1, chunks)
         cross = mx_ref[chunk + 1]
         dz = chain(chunk, dz_after, cross)
@@ -541,6 +563,9 @@
     dw_ref[...] += lam_w + add_w
     dc_ref[...] += lam_c + add_c
     finish(0)
+    exchange.end()
+    for total in sums:
+        total.end()
     gather.end()
 
 
@@ -582,13 +607,13 @@
         ]
         + gather_scratch(),
         compiler_params=pltpu.CompilerParams(
-            collective_id=number, has_side_effects=True, vmem_limit_bytes=20 * 1024 * 1024
+            collective_id=number, has_side_effects=True, vmem_limit_bytes=MOST_VMEM
         ),
         name="inner_forward",
     )(starts, proj, rates, ttt_w, ttt_b, gain, shift, own)
 
 
-def inner_backward(starts, proj, rates, d_inner, d_gate, own, kept, number):
+def inner_backward(starts, proj, rates, d_inner, d_gate, mixed, grads, own, kept, number):
     tokens = proj.shape[0]
     chunks = tokens // CHUNK
     square = jax.ShapeDtypeStruct((HD, LANES), F32)
@@ -614,24 +639,29 @@
             cell,
             cell16,
             cell,
+            jax.ShapeDtypeStruct((tokens, LANES), BF16),
+            *(jax.ShapeDtypeStruct(grad.shape, BF16) for grad in grads),
             gathered_shape(own),
         ],
         in_specs=[pl.BlockSpec(memory_space=pltpu.SMEM)]
-        + whole_vmem(4)
+        + whole_vmem(7)
         + [ANYWHERE]
         + whole_vmem(len(kept)),
-        out_specs=whole_vmem(17) + [ANYWHERE],
+        out_specs=whole_vmem(20) + [ANYWHERE],
         scratch_shapes=[
             pltpu.VMEM((LANES, LANES), F32),
             pltpu.VMEM((LANES, LANES), F32),
             pltpu.VMEM((LANES, LANES), F32),
         ]
+        + to_heads_scratch(2)
+        + seq_sum_scratch(grads[0].shape, 0)
+        + seq_sum_scratch(grads[1].shape, 1)
         + gather_scratch(),
         compiler_params=pltpu.CompilerParams(
-            collective_id=number, has_side_effects=True, vmem_limit_bytes=24 * 1024 * 1024
+            collective_id=number, has_side_effects=True, vmem_limit_bytes=MOST_VMEM
         ),
         name="inner_backward",
-    )(starts, proj, rates, d_inner, d_gate, own, *kept)
+    )(starts, proj, rates, d_inner, d_gate, mixed, *grads, own, *kept)
 
 
 def heads_of_lanes(values):
@@ -671,7 +701,7 @@
             pl.BlockSpec((block, columns), lambda i: (i, 0)),
             pl.BlockSpec((block // CHUNK, 1, LANES), lambda i: (i, 0, 0)),
         ],
-        compiler_params=pltpu.CompilerParams(vmem_limit_bytes=12 * 1024 * 1024),
+        compiler_params=pltpu.CompilerParams(vmem_limit_bytes=MOST_VMEM),
         name="project",
     )(gathered, w_in, rate_w, bias)
 
@@ -901,8 +931,8 @@
         first, second = first % RING_X, second % RING_X
         return (first, second) if axis == 0 else (second, first)
 
-    def start(self):
-        greet([{"head": peer} for peer in self.near.values()])
+    def start(self, greeted=None):
+        greet(greeted or [{"head": peer} for peer in self.near.values()])
         self.own_copy().start()
         for turned in (False, True):
             for axis, units in self.halves:
@@ -990,8 +1020,179 @@
     )(own)
 
 
+class SeqSum:
+    SENDS = 24
+
+    def __init__(
+        self, axis, part_ref, sum_ref, pair_held, ring_held, stage_ref, send_sem, recv_sem
+    ):
+        self.axis = axis
+        self.part_ref, self.sum_ref = part_ref, sum_ref
+        self.pair_held, self.ring_held, self.stage_ref = pair_held, ring_held, stage_ref
+        self.send_sem, self.recv_sem = send_sem, recv_sem
+        seq = lax.axis_index("seq")
+        self.chips = lax.axis_size("seq") // 2
+        self.z, self.core = seq // 2, lax.rem(seq, 2)
+        self.quarter = part_ref.shape[axis] // (2 * self.chips)
+        self.unit = self.quarter // 2
+        self.sibling = self.z * 2 + 1 - self.core
+        self.near = {
+            way: lax.rem(self.z + way + self.chips, self.chips) * 2 + self.core for way in (1, -1)
+        }
+        self.sends = []
+        self.steps = [self.pair_arrivals, self.far_arrivals, self.own_sum, self.ring_arrivals]
+
+    def peers(self):
+        return [{"seq": peer} for peer in (self.sibling, self.near[1], self.near[-1])]
+
+    def cut(self, ref, start, size):
+        if not isinstance(start, int):
+            start = pl.multiple_of(start, size)
+        return ref.at[pl.ds(start, size)] if self.axis == 0 else ref.at[:, pl.ds(start, size)]
+
+    def part(self, ref, core, dz, unit=None):
+        owner = lax.rem(self.z + dz + self.chips, self.chips)
+        start = (core * self.chips + owner) * self.quarter
+        if unit is None:
+            return self.cut(ref, start, self.quarter)
+        return self.cut(ref, start + unit * self.unit, self.unit)
+
+    def paired(self, dz):
+        return self.cut(self.pair_held, dz * self.quarter, self.quarter)
+
+    def staged(self, dz, unit=None):
+        if unit is None:
+            return self.cut(self.stage_ref, dz * self.quarter, self.quarter)
+        return self.cut(self.stage_ref, dz * self.quarter + unit * self.unit, self.unit)
+
+    def held(self, number):
+        return self.cut(self.ring_held, number * self.unit, self.unit)
+
+    def send(self, source, target, peer):
+        number = len(self.sends)
+
+        def copy():
+            return pltpu.make_async_remote_copy(
+                src_ref=source(),
+                dst_ref=target(),
+                send_sem=self.send_sem.at[number],
+                recv_sem=self.recv_sem.at[number],
+                device_id={"seq": peer},
+                device_id_type=MESH,
+            )
+
+        copy().start()
+        self.sends.append(copy)
+        return number
+
+    def arrive(self, number):
+        self.sends[number]().wait_recv()
+
+    def start(self):
+        self.pair = {}
+        for dz in (2, 1, 3, 0):
+            self.pair[dz] = self.send(
+                partial(self.part, self.part_ref, 1 - self.core, dz),
+                partial(self.paired, dz),
+                self.sibling,
+            )
+
+    def pair_arrivals(self):
+        for dz in (2, 1, 3, 0):
+            self.arrive(self.pair[dz])
+            total = self.part(self.part_ref, self.core, dz)[...].astype(F32)
+            total = total + self.paired(dz)[...].astype(F32)
+            self.staged(dz)[...] = total.astype(BF16)
+            if dz == 2:
+                self.far = {
+                    way: self.send(
+                        partial(self.staged, 2, unit), partial(self.held, unit), self.near[way]
+                    )
+                    for way, unit in ((1, 0), (-1, 1))
+                }
+        self.plain = {
+            way: self.send(
+                partial(self.staged, way % 4, unit), partial(self.held, 2 + unit), self.near[way]
+            )
+            for way, unit in ((1, 1), (-1, 0))
+        }
+
+    def far_arrivals(self):
+        self.onward = {}
+        for way, unit in ((1, 0), (-1, 1)):
+            self.arrive(self.far[way])
+            place = self.staged(way % 4, unit)
+            total = place[...].astype(F32) + self.held(unit)[...].astype(F32)
+            place[...] = total.astype(BF16)
+            self.onward[way] = self.send(
+                partial(self.staged, way % 4, unit), partial(self.held, 4 + unit), self.near[way]
+            )
+
+    def own_sum(self):
+        for way in (1, -1):
+            self.arrive(self.plain[way])
+            self.arrive(self.onward[way])
+        self.direct = {}
+        for unit in (0, 1):
+            total = self.staged(0, unit)[...].astype(F32)
+            total = total + self.held(2 + unit)[...].astype(F32)
+            total = total + self.held(4 + unit)[...].astype(F32)
+            place = self.part(self.sum_ref, self.core, 0, unit)
+            place[...] = total.astype(BF16)
+        for unit in (0, 1):
+            place = partial(self.part, self.sum_ref, self.core, 0, unit)
+            for way in (1, -1):
+                self.direct[way, unit] = self.send(place, place, self.near[way])
+        self.relayed = [self.relay(0, unit) for unit in (0, 1)]
+
+    def relay(self, dz, unit):
+        place = partial(self.part, self.sum_ref, self.core, dz, unit)
+        return self.send(place, place, self.sibling)
+
+    def ring_arrivals(self):
+        self.passed = {}
+        for unit in (0, 1):
+            for way in (1, -1):
+                self.arrive(self.direct[way, unit])
+                if unit == (0 if way == 1 else 1):
+                    place = partial(self.part, self.sum_ref, self.core, -way, unit)
+                    self.passed[way] = self.send(place, place, self.near[way])
+        for unit in (0, 1):
+            for way in (1, -1):
+                self.relayed.append(self.relay(-way, unit))
+
+    def end(self):
+        for way, unit in ((1, 0), (-1, 1)):
+            self.arrive(self.passed[way])
+            self.relayed.append(self.relay(2, unit))
+        for number in self.relayed:
+            self.arrive(number)
+        for copy in self.sends:
+            copy().wait_send()
+
+
+def seq_sum_scratch(shape, axis):
+    def pieces(numerator, denominator):
+        size = numerator * shape[axis] // denominator
+        return pltpu.VMEM((size, shape[1]) if axis == 0 else (shape[0], size), BF16)
+
+    return [
+        pieces(1, 2),
+        pieces(6, 16),
+        pieces(1, 2),
+        pltpu.SemaphoreType.DMA((SeqSum.SENDS,)),
+        pltpu.SemaphoreType.DMA((SeqSum.SENDS,)),
+    ]
+
+
+SEQ_SUM_SCRATCH = 5
+
+
 class SmallSums:
-    def __init__(self, shard_ref, shard_out, lines_out, held, send_sem, recv_sem, *line_sems):
+    def __init__(
+        self, sums, shard_ref, shard_out, lines_out, held, send_sem, recv_sem, *line_sems
+    ):
+        self.sums = sums
         self.shard_ref, self.shard_out, self.lines_out = shard_ref, shard_out, lines_out
         self.held, self.send_sem, self.recv_sem = held, send_sem, recv_sem
         self.line_send, self.line_recv = line_sems
@@ -1006,7 +1207,13 @@
             {"head": peer} for peer in self.head_peers
         ]
 
+    def step(self, index):
+        for total in self.sums:
+            total.steps[index]()
+
     def start(self):
+        for total in self.sums:
+            total.start()
         self.sends = []
         for ahead, peer in enumerate(self.seq_peers, 1):
             done = pltpu.make_async_remote_copy(
@@ -1042,64 +1249,69 @@
             self.passed.append(done)
 
     def end(self):
+        for total in self.sums:
+            total.end()
         for done in self.passed:
             done.wait_recv()
         for done in self.sends + self.passed:
             done.wait_send()
 
 
-def everywhere_kernel(part_ref, sum_ref, seq_held, line_ref, head_held, *sems):
-    head, seq = lax.axis_index("head"), lax.axis_index("seq")
-    seqs = seq_held.shape[0]
-    seq_peers = [lax.rem(seq + ahead, seqs) for ahead in range(1, seqs)]
-    head_peers = [lax.rem(head + ahead, GROUP) for ahead in range(1, GROUP)]
-    greet([{"seq": peer} for peer in seq_peers] + [{"head": peer} for peer in head_peers])
-
-    def exchange(source, held, axis, peers, send_sem, recv_sem):
+class Everywhere:
+    def __init__(self, part_ref, sum_ref, seq_held, line_ref, head_held, *sems):
+        self.part_ref, self.sum_ref = part_ref, sum_ref
+        self.seq_held, self.line_ref, self.head_held = seq_held, line_ref, head_held
+        self.sems = sems
+
+    def push(self, source, held, axis, send_sem, recv_sem):
+        count, me = held.shape[0], lax.axis_index(axis)
         sends = []
-        for ahead, peer in enumerate(peers, 1):
+        for ahead in range(1, count):
             done = pltpu.make_async_remote_copy(
                 src_ref=source,
                 dst_ref=held.at[ahead],
                 send_sem=send_sem.at[ahead],
                 recv_sem=recv_sem.at[ahead],
-                device_id={axis: peer},
+                device_id={axis: lax.rem(me + ahead, count)},
                 device_id_type=MESH,
             )
             done.start()
             sends.append(done)
+        return sends
+
+    def total(self, source, held, sends):
         total = source[...]
         for ahead, done in enumerate(sends, 1):
             done.wait_recv()
             total = total + held[ahead]
-        return total, sends
-
-    line_ref[...], sends = exchange(part_ref, seq_held, "seq", seq_peers, *sems[:2])
-    sum_ref[...], passed = exchange(line_ref, head_held, "head", head_peers, *sems[2:])
-    for done in sends + passed:
-        done.wait_send()
-
-
-def sum_everywhere(part, seqs, number):
-    return pl.pallas_call(
-        everywhere_kernel,
-        out_shape=jax.ShapeDtypeStruct(part.shape, F32),
-        in_specs=whole_vmem(1),
-        out_specs=pl.BlockSpec(memory_space=pltpu.VMEM),
-        scratch_shapes=[
-            pltpu.VMEM((seqs,) + part.shape, F32),
-            pltpu.VMEM(part.shape, F32),
-            pltpu.VMEM((GROUP,) + part.shape, F32),
-            pltpu.SemaphoreType.DMA((seqs,)),
-            pltpu.SemaphoreType.DMA((seqs,)),
-            pltpu.SemaphoreType.DMA((GROUP,)),
-            pltpu.SemaphoreType.DMA((GROUP,)),
-        ],
-        compiler_params=pltpu.CompilerParams(
-            collective_id=number, has_side_effects=True, vmem_limit_bytes=4 * 1024 * 1024
-        ),
-        name="sum_everywhere",
-    )(part)
+        return total
+
+    def start(self):
+        self.over_seq = self.push(self.part_ref, self.seq_held, "seq", *self.sems[:2])
+
+    def turn(self):
+        self.line_ref[...] = self.total(self.part_ref, self.seq_held, self.over_seq)
+        self.over_head = self.push(self.line_ref, self.head_held, "head", *self.sems[2:])
+
+    def end(self):
+        self.sum_ref[...] = self.total(self.line_ref, self.head_held, self.over_head)
+        for done in self.over_seq + self.over_head:
+            done.wait_send()
+
+
+def everywhere_scratch(shape, seqs):
+    return [
+        pltpu.VMEM((seqs,) + shape, F32),
+        pltpu.VMEM(shape, F32),
+        pltpu.VMEM((GROUP,) + shape, F32),
+        pltpu.SemaphoreType.DMA((seqs,)),
+        pltpu.SemaphoreType.DMA((seqs,)),
+        pltpu.SemaphoreType.DMA((GROUP,)),
+        pltpu.SemaphoreType.DMA((GROUP,)),
+    ]
+
+
+EVERYWHERE_SCRATCH = 7
 
 
 def scatter_kernel(part_ref, sum_ref, held_ref, stage_ref, send_sem, recv_sem):
@@ -1109,17 +1321,49 @@
 def scatter_small_kernel(
     part_ref,
     shard_ref,
-    sum_ref,
+    grad_in_ref,
+    grad_out_ref,
+    tokens_ref,
+    d_res_ref,
+    gain_ref,
+    grad_tokens_ref,
+    gain_sum_ref,
     shard_out,
     lines_out,
+    sum_in_ref,
+    sum_out_ref,
     held_ref,
     stage_ref,
     send_sem,
     recv_sem,
+    sum_ref,
+    gain_part_ref,
     *scratch,
 ):
-    small = SmallSums(shard_ref, shard_out, lines_out, *scratch)
+    count = 2 * SEQ_SUM_SCRATCH
+    sums = (
+        SeqSum(0, grad_in_ref, sum_in_ref, *scratch[:SEQ_SUM_SCRATCH]),
+        SeqSum(1, grad_out_ref, sum_out_ref, *scratch[SEQ_SUM_SCRATCH:count]),
+    )
+    more = count + EVERYWHERE_SCRATCH
+    gain_sum = Everywhere(gain_part_ref, gain_sum_ref, *scratch[count:more])
+    small = SmallSums(sums, shard_ref, shard_out, lines_out, *scratch[more:])
     scatter_body(small, part_ref, sum_ref, held_ref, stage_ref, send_sem, recv_sem)
+    resid = tokens_ref[...].astype(F32)
+    scale = lax.rsqrt(mean_columns(resid * resid) + EPS)
+    normed = resid * scale
+    d_norm = sum_ref[...]
+    line = sum_rows(d_norm * normed)
+    for k in range(GROUP):
+        gain_part_ref[k : k + 1, :] = line[:, k * LANES : (k + 1) * LANES]
+    gain_sum.start()
+    weighted = d_norm * gain_ref[...]
+    grad_tokens_ref[...] = d_res_ref[...] + scale * (
+        weighted - normed * mean_columns(weighted * normed)
+    )
+    gain_sum.turn()
+    small.end()
+    gain_sum.end()
 
 
 def scatter_body(small, part_ref, sum_ref, held_ref, stage_ref, send_sem, recv_sem):
@@ -1206,9 +1450,12 @@
     plains = {(axis, o): plain(axis, units, o) for o in order for axis, units in halves}
     if small is not None:
         small.start()
+        small.step(0)
     onwards = {
         (axis, o): onward(axis, units, o, fars[axis, o]) for o in order for axis, units in halves
     }
+    if small is not None:
+        small.step(1)
     last_far, last_plain, last_onward = {}, {}, {}
 
     def first_sum(axis, units, other):
@@ -1224,9 +1471,12 @@
         first_sum(axis, units, 1)
         first_sum(axis, units, 3)
         last_plain[axis] = plain(1 - axis, units, 0)
+    if small is not None:
+        small.step(2)
     for axis, units in halves:
         last_onward[axis] = onward(1 - axis, units, 0, last_far[axis])
     if small is not None:
+        small.step(3)
         small.turn()
     for axis, units in halves:
         own = collect(axis, units, 0, plains[axis, 0], onwards[axis, 0])
@@ -1240,8 +1490,6 @@
             sum_ref[pl.ds(unit * unit_rows, unit_rows), :] = total
     for done in sends:
         done.wait_send()
-    if small is not None:
-        small.end()
 
 
 def scatter_scratch(rows, width):
@@ -1268,18 +1516,25 @@
     )(part)
 
 
-def scatter_rows_and_small(part, shard, seqs, number):
-    rows, width = part.shape[0] // GROUP, part.shape[1]
+def scatter_rows_and_small(part, shard, grads, tokens, d_res, gain, seqs, number):
+    rows, width = tokens.shape
+    lines = (GROUP, width // GROUP)
     return pl.pallas_call(
         scatter_small_kernel,
         out_shape=[
             jax.ShapeDtypeStruct((rows, width), F32),
+            jax.ShapeDtypeStruct(lines, F32),
             jax.ShapeDtypeStruct(shard.shape, F32),
             jax.ShapeDtypeStruct((GROUP, 8, LANES), F32),
+            *(jax.ShapeDtypeStruct(grad.shape, BF16) for grad in grads),
         ],
-        in_specs=whole_vmem(2),
-        out_specs=whole_vmem(3),
+        in_specs=whole_vmem(7),
+        out_specs=whole_vmem(6),
         scratch_shapes=scatter_scratch(rows, width)
+        + [pltpu.VMEM((rows, width), F32), pltpu.VMEM(lines, F32)]
+        + seq_sum_scratch(grads[0].shape, 0)
+        + seq_sum_scratch(grads[1].shape, 1)
+        + everywhere_scratch(lines, seqs)
         + [
             pltpu.VMEM((seqs,) + shard.shape, F32),
             pltpu.SemaphoreType.DMA((seqs,)),
@@ -1288,10 +1543,10 @@
             pltpu.SemaphoreType.DMA((GROUP,)),
         ],
         compiler_params=pltpu.CompilerParams(
-            collective_id=number, has_side_effects=True, vmem_limit_bytes=28 * 1024 * 1024
+            collective_id=number, has_side_effects=True, vmem_limit_bytes=48 * 1024 * 1024
         ),
         name="scatter_rows_and_small",
-    )(part, shard)
+    )(part, shard, *grads, tokens, d_res, gain)
 
 
 def to_tokens_kernel(
@@ -1368,79 +1623,90 @@
     )(inner, gate, gains)
 
 
-def to_heads_kernel(
-    inner_ref,
-    gate_ref,
-    mixed_ref,
-    sums_ref,
-    inner_out,
-    gate_out,
-    mixed_out,
-    sums_out,
-    send_sem,
-    recv_sem,
-    local_sem,
-):
-    head = lax.axis_index("head")
-    rows = inner_ref.shape[0]
-    triples = ((inner_ref, inner_out), (gate_ref, gate_out), (mixed_ref, mixed_out))
-
-    def rows_of(index):
-        return pl.ds(pl.multiple_of(index * rows, rows), rows)
-
-    def columns_of(index):
+class ToHeads:
+    def __init__(self, pairs, send_sem, recv_sem):
+        self.pairs, self.send_sem, self.recv_sem = pairs, send_sem, recv_sem
+        self.head = lax.axis_index("head")
+        self.rows = pairs[0][0].shape[0]
+        self.peers = [lax.rem(self.head + ahead, GROUP) for ahead in range(1, GROUP)]
+
+    def rows_of(self, index):
+        return pl.ds(pl.multiple_of(index * self.rows, self.rows), self.rows)
+
+    def columns_of(self, index):
         return pl.ds(pl.multiple_of(index * LANES, LANES), LANES)
 
-    def jobs(peer):
-        return [
-            (source.at[:, columns_of(peer)], target.at[rows_of(head)]) for source, target in triples
-        ] + [(sums_ref.at[peer], sums_out.at[head])]
-
-    mine = [
-        pltpu.make_async_copy(source, target, local_sem.at[index])
-        for index, (source, target) in enumerate(jobs(head))
+    def start(self):
+        self.sends = []
+        for ahead, peer in enumerate(self.peers, 1):
+            for index, (source, target, first) in enumerate(self.pairs):
+                done = pltpu.make_async_remote_copy(
+                    src_ref=source.at[:, self.columns_of(peer)],
+                    dst_ref=target.at[self.rows_of(self.head), first : first + LANES],
+                    send_sem=self.send_sem.at[ahead, index],
+                    recv_sem=self.recv_sem.at[ahead, index],
+                    device_id={"head": peer},
+                    device_id_type=MESH,
+                )
+                done.start()
+                self.sends.append(done)
+        for source, target, first in self.pairs:
+            target[self.rows_of(self.head), first : first + LANES] = source[
+                :, self.columns_of(self.head)
+            ]
+
+    def end(self):
+        for done in self.sends:
+            done.wait()
+
+
+def to_heads_scratch(arrays):
+    return [
+        pltpu.SemaphoreType.DMA((GROUP, arrays)),
+        pltpu.SemaphoreType.DMA((GROUP, arrays)),
     ]
-    for done in mine:
+
+
+def to_heads_kernel(inner_ref, sums_ref, inner_out, sums_out, send_sem, recv_sem, *sums_sems):
+    exchange = ToHeads([(inner_ref, inner_out, 0)], send_sem, recv_sem)
+    head = exchange.head
+    greet([{"head": peer} for peer in exchange.peers])
+    exchange.start()
+    sends = []
+    for ahead, peer in enumerate(exchange.peers, 1):
+        done = pltpu.make_async_remote_copy(
+            src_ref=sums_ref.at[peer],
+            dst_ref=sums_out.at[head],
+            send_sem=sums_sems[0].at[ahead],
+            recv_sem=sums_sems[1].at[ahead],
+            device_id={"head": peer},
+            device_id_type=MESH,
+        )
         done.start()
-    greet([{"head": lax.rem(head + ahead, GROUP)} for ahead in range(1, GROUP)])
-    sends = []
-    for ahead in range(1, GROUP):
-        peer = lax.rem(head + ahead, GROUP)
-        for index, (source, target) in enumerate(jobs(peer)):
-            done = pltpu.make_async_remote_copy(
-                src_ref=source,
-                dst_ref=target,
-                send_sem=send_sem.at[ahead, index],
-                recv_sem=recv_sem.at[ahead, index],
-                device_id={"head": peer},
-                device_id_type=MESH,
-            )
-            done.start()
-            sends.append(done)
-    for done in mine:
-        done.wait()
+        sends.append(done)
+    sums_out[head] = sums_ref[head]
+    exchange.end()
     for done in sends:
         done.wait()
 
 
-def to_heads(inner, gate, mixed, sums, number):
+def to_heads(inner, sums, number):
     rows = inner.shape[0]
-    tall = jax.ShapeDtypeStruct((rows * GROUP, LANES), BF16)
     return pl.pallas_call(
         to_heads_kernel,
-        out_shape=[tall, tall, tall, jax.ShapeDtypeStruct(sums.shape, F32)],
-        in_specs=whole_vmem(4),
-        out_specs=whole_vmem(4),
-        scratch_shapes=[
-            pltpu.SemaphoreType.DMA((GROUP, 4)),
-            pltpu.SemaphoreType.DMA((GROUP, 4)),
-            pltpu.SemaphoreType.DMA((4,)),
+        out_shape=[
+            jax.ShapeDtypeStruct((rows * GROUP, LANES), BF16),
+            jax.ShapeDtypeStruct(sums.shape, F32),
         ],
+        in_specs=whole_vmem(2),
+        out_specs=whole_vmem(2),
+        scratch_shapes=to_heads_scratch(1)
+        + [pltpu.SemaphoreType.DMA((GROUP,)), pltpu.SemaphoreType.DMA((GROUP,))],
         compiler_params=pltpu.CompilerParams(
             collective_id=number, has_side_effects=True, vmem_limit_bytes=8 * 1024 * 1024
         ),
         name="to_heads",
-    )(inner, gate, mixed, sums)
+    )(inner, sums)
 
 
 def after(value, *others):
@@ -1504,17 +1770,18 @@
     up_part = gate_up[:, ffn_local:].astype(F32)
     silu_val, silu_pull = jax.vjp(jax.nn.silu, gate_part)
     hidden_state = (silu_val * up_part).astype(BF16)
-    ffn_part = dot_nn(hidden_state, w_down).astype(BF16)
+    half = width // 2
+    ffn_first = dot_nn(hidden_state, w_down[:, :half]).astype(BF16)
+    out_first = lax.psum_scatter(ffn_first, "head", scatter_dimension=0, tiled=True)
+    cot_rows = after(cot_rows, ffn_first)
     d_hidden = dot_nt(cot_rows, w_down)
     d_gate_part = silu_pull(d_hidden * up_part)[0]
     d_gate_up = jnp.concatenate([d_gate_part, d_hidden * silu_val], axis=1).astype(BF16)
     grad_w_down = dot_tn(hidden_state, cot_rows).astype(BF16)
-    grad_w_gate_up = dot_tn(ffn_rows, d_gate_up).reshape(width, 2, ffn_local).astype(BF16)
+    grad_w_down = jnp.pad(grad_w_down, ((0, -ffn_local % 16), (0, 0)))
+    grad_w_gate_up = dot_tn(ffn_rows, d_gate_up).astype(BF16)
     d_norm_part = dot_nt(d_gate_up, w_gu_flat).astype(BF16)
-    d_norm_two = scatter_rows(after(d_norm_part, grad_w_down, grad_w_gate_up, ffn_part), 3)
-    ffn_out = lax.psum_scatter(
-        after(ffn_part, d_norm_two), "head", scatter_dimension=0, tiled=True
-    )
+    d_norm_two = scatter_rows(after(d_norm_part, grad_w_down, grad_w_gate_up), 3)
 
     d_res, d_mix, d_inner_tok, d_gate_tok, token_sums = middle_backward(
         d_norm_two,
@@ -1526,24 +1793,43 @@
         all_gains,
         w_out_all,
     )
-    d_inner, d_gate, mixed_in, head_sums = to_heads(
-        d_inner_tok, d_gate_tok, mixed_tok, token_sums, 4
+    d_inner, head_sums = to_heads(d_inner_tok, token_sums, 4)
+    head_sums = jnp.sum(head_sums, axis=0)
+
+    (
+        d_projected,
+        d_bias,
+        d_start_w,
+        d_start_c,
+        d_gain,
+        d_shift,
+        *_,
+        mixed_in,
+        sum_w_gate_up,
+        sum_w_down,
+        mix_rows,
+    ) = inner_backward(
+        doc_starts,
+        projected,
+        rate_lanes,
+        after(d_inner, out_first),
+        d_gate_tok,
+        mixed_tok,
+        (grad_w_gate_up, grad_w_down),
+        d_mix,
+        kept,
+        8,
     )
-    head_sums = jnp.sum(head_sums, axis=0)
-    output = (hidden_res + ffn_out.astype(F32)).astype(BF16)
-
-    d_projected, d_bias, d_start_w, d_start_c, d_gain, d_shift, *_, mix_rows = inner_backward(
-        doc_starts, projected, rate_lanes, d_inner, d_gate, d_mix, kept, 8
-    )
-    grad_in = dot_tn(gathered, d_projected)
+    ffn_second = dot_nn(after(hidden_state, d_projected), w_down[:, half:]).astype(BF16)
+    out_second = lax.psum_scatter(ffn_second, "head", scatter_dimension=0, tiled=True)
+    ffn_out = jnp.concatenate([out_first, out_second], axis=1).astype(F32)
+    output = (hidden_res + ffn_out).astype(BF16)
+    grad_in = dot_tn(after(gathered, ffn_second), d_projected)
     w_columns = jnp.pad(w_rate, ((0, 0), (0, local_width - head_count)))
     w_columns = jnp.concatenate([w_in_flat, w_columns], axis=1)
     grad_w_rate = grad_in[:, 4 * local_width : 4 * local_width + head_count]
-    grad_w_in = grad_in[:, : 4 * local_width].astype(BF16).reshape(width, 4, local_width)
+    grad_w_in = grad_in[:, : 4 * local_width].astype(BF16)
     grad_w_out = dot_tn(mixed_in, mix_rows).astype(BF16)
-    sum_w_in, sum_w_out, sum_w_down, sum_w_gate_up = lax.psum(
-        after((grad_w_in, grad_w_out, grad_w_down, grad_w_gate_up), ffn_out), "seq"
-    )
     singles = jnp.stack(
         [
             head_sums[2],
@@ -1559,25 +1845,24 @@
     rate_rows = grad_w_rate.T.reshape(2 * width // LANES, LANES)
     shard = jnp.concatenate([singles, d_start_w, rate_rows], axis=0)
     d_norm_part = dot_nt(d_projected, w_columns).astype(BF16)
-    d_norm_one, shard, lines = scatter_rows_and_small(
-        after(d_norm_part, grad_w_in, grad_w_out), shard, seqs, 5
+    grad_tokens, sum_norm_gain, shard, lines, sum_w_in, sum_w_out = scatter_rows_and_small(
+        d_norm_part,
+        shard,
+        (grad_w_in, grad_w_out),
+        tokens,
+        d_res,
+        norm_gain[None],
+        seqs,
+        5,
     )
-    weighted = d_norm_one * norm_gain
-    normed = resid * scale_one
-    grad_tokens = d_res + scale_one * (
-        weighted - normed * jnp.mean(weighted * normed, axis=-1, keepdims=True)
-    )
-
-    grad_norm_gain = jnp.sum(d_norm_one * normed, axis=0).reshape(GROUP, LANES)
-    sum_norm_gain = sum_everywhere(grad_norm_gain, seqs, 6).reshape(width)
     sum_ffn_gain = lines[:, 0].reshape(width)
     sum_ttt_w = shard[8 : 8 + head_dim].reshape(head_dim, head_count, head_dim)
     per_head = (head_count, head_dim)
     return (
         output,
         grad_tokens,
-        sum_norm_gain,
-        sum_w_in.astype(F32),
+        sum_norm_gain.reshape(width),
+        sum_w_in.astype(F32).reshape(width, 4, local_width),
         shard[8 + head_dim :].reshape(head_count, width).T,
         jnp.sum(shard[6].reshape(per_head), axis=1),
         sum_ttt_w.transpose(1, 2, 0),
@@ -1588,8 +1873,8 @@
         shard[2],
         sum_w_out.astype(F32),
         sum_ffn_gain,
-        sum_w_gate_up.astype(F32),
-        sum_w_down.astype(F32),
+        sum_w_gate_up.astype(F32).reshape(width, 2, ffn_local),
+        sum_w_down[:ffn_local].astype(F32),
     )
 
 

time: 583 us -> 570 us (0.978)
  Pallas kernels: 400 us -> 414 us
  waiting for transfers between devices: 13.9 us -> 0.05 us
  local copies, waits for them, and re-layouts: 62 us -> 48.3 us
  matrix products: 64.7 us -> 72.1 us
    pallas_call x2 -> x1, Pallas kernels: 40.5 us -> 10.2 us  [to_heads(): pl.pallas_call(to_heads_kernel, out_shape=[jax.ShapeDtypeStruct((rows * G...]
    unnamed x131 -> x113, local copies, waits for them, and re-layouts: 47.1 us -> 29.5 us
    pallas_call x1, Pallas kernels: 55.4 us -> 71.2 us  [scatter_rows_and_small(): pl.pallas_call(scatter_small_kernel, out_shape=[jax.ShapeDtypeStruct((row...]
    psum x1 -> x0, waiting for transfers between devices: 13.9 us -> none  [per_device(): lax.psum(after((grad_w_in, grad_w_out, grad_w_down, grad_w_gate_up), ffn_...]
    pallas_call x1, Pallas kernels: 44.3 us -> 58.1 us  [scatter_rows(): pl.pallas_call(scatter_kernel, out_shape=jax.ShapeDtypeStruct((rows, widt...]
    reshape x0 -> x2, local copies, waits for them, and re-layouts: none -> 8.12 us  [the longest x1 5.17 us: per_device(): sum_w_gate_up.astype(F32).reshape(width, 2, ffn_local)]
    pallas_call x1, Pallas kernels: 80.8 us -> 88 us  [inner_backward(): pl.pallas_call(backward_kernel, out_shape=[jax.ShapeDtypeStruct((tokens,...]
    dot_general x2 -> x3, matrix products: 15.6 us -> 17.4 us  [dot_nn(): lax.dot_general(a, b, (((1,), (0,)), ((), ())), preferred_element_type=F32)]
  transfers between devices with their start and end apart: 3 -> 3, of which waited for: 1 -> 0; matrix products, arithmetic and copies ran while one was open for 6% -> 16% of each run, Pallas kernels for 53% -> 49%
where the time goes in v1:
time: 570 us; the launch traced here: 561 us
  Pallas kernels  414 us (73%)
  matrix products  72.1 us (13%)
  local copies, waits for them, and re-layouts  48.3 us (8%)
  between operations  14.8 us (3%)
  other arithmetic  11.9 us (2%)
    pallas_call x2, Pallas kernels, gather_rows(): pl.pallas_call(gather_kernel, out_shape=gathered_shape(own), in_specs=[AN...  102 us
    pallas_call x1, Pallas kernels, inner_backward(): pl.pallas_call(backward_kernel, out_shape=[jax.ShapeDtypeStruct((tokens,...  88 us
    pallas_call x1, Pallas kernels, scatter_rows_and_small(): pl.pallas_call(scatter_small_kernel, out_shape=[jax.ShapeDtypeStruct((row...  71.2 us
    pallas_call x1, Pallas kernels, scatter_rows(): pl.pallas_call(scatter_kernel, out_shape=jax.ShapeDtypeStruct((rows, widt...  58.1 us
    pallas_call x1, Pallas kernels, inner_forward(): pl.pallas_call(forward_kernel, out_shape=[jax.ShapeDtypeStruct((tokens, L...  50.5 us
    dot_general x4, matrix products, dot_tn(): lax.dot_general(a, b, (((0,), (0,)), ((), ())), preferred_element_type=F32)  29.8 us
    unnamed x113, local copies, waits for them, and re-layouts  29.5 us
    dot_general x3, matrix products, dot_nt(): lax.dot_general(a, b, (((1,), (1,)), ((), ())), preferred_element_type=F32)  24.8 us
  transfers between devices with their start and end apart: 3, of which 0 were waited for; matrix products, arithmetic and copies ran while one was open for 16% of the time, Pallas kernels for 49%

profile of v1, /device:TPU:1, one launch (start us, length us, event | category | flops | bytes accessed | tf_op | source)
XLA Modules:
  0.0 561.2 jit_solution(10879680374484595099)
XLA Ops:
  7.2 1.6 constant_dynamic-slice_fusion
  10.2 2.0 fusion.16.refs_0_
  12.2 53.4 %gather_rows.2.x_ref = bf16[2048,2048]{1,0:T(8,128)(2,1)} custom-call(bf16[128,2048]{1,0:T(8,128)(2,1)} %fusion.16.refs_0_), custom_call_target="tpu_custom_call" | custom-call | tf_op jit(solution)/shard_map/gather_rows/pallas_call | solution.py:1012
  65.6 3.3 copy.58
  70.3 11.9 %project.1 = (bf16[2048,512]{1,0:T(8,128)(2,1)}, f32[32,1,128]{2,1,0:T(1,128)}) custom-call(bf16[2048,2048]{1,0:T(8,128)(2,1)} %gather_rows.2.x_ref, bf16[2048,512]{1,0:T(8,128)(2,1)} %bitcast.54, bf16[16,2048]{1,0:T(8,128)(2,1)} %pad.12.rate_w_ref, f32[1,128]{1,0:T(1,128)} %broadcast_in_dim_reshape.3.bias_ref), custom_call_target="tpu_custom_call" | custom-call | tf_op jit(solution)/shard_map/project/pallas_call | solution.py:687
  82.2 50.5 %inner_forward.1 = (bf16[2048,128]{1,0:T(8,128)(2,1)}, f32[32,64,128]{2,1,0:T(8,128)}, f32[32,64,128]{2,1,0:T(8,128)}, f32[32,64,128]{2,1,0:T(8,128)}, f32[33,64...) custom-call(s32[1,3]{1,0:T(1,128)} %starts_ref.3, ...), custom_call_target="tpu_custom_call" | custom-call | tf_op jit(solution)/shard_map/inner_forward/pallas_call | solution.py:581
  133.9 16.0 %to_tokens.1 = (bf16[128,2048]{1,0:T(8,128)(2,1)S(1)}, bf16[128,2048]{1,0:T(8,128)(2,1)S(1)}, f32[16,8,128]{2,1,0:T(8,128)S(1)}) custom-call(bf16[2048,128]{1,0:T(8,128)(2,1)S(1)} %copy-done.22, bf16[2048,512]{1,0:T(8,128)(2,1)S(1)} %copy-done.3, f32[8,128]{1,0:T(8,128)S(1)} %maximum_maximum_fusion.gains_ref), custom_call_target="tpu_custom_call" | custom-call | tf_op jit(solution)/shard_map/to_tokens/pallas_call | solution.py:1609
  151.5 3.4 copy-done.2
  157.0 1.9 middle_forward.1
  161.5 48.4 %gather_rows.3 = bf16[2048,2048]{1,0:T(8,128)(2,1)} custom-call(bf16[128,2048]{1,0:T(8,128)(2,1)} %copy-done.25), custom_call_target="tpu_custom_call" | custom-call | tf_op jit(solution)/shard_map/gather_rows/pallas_call | solution.py:1012
  209.8 8.6 %convolution_convert_fusion.5 = bf16[2048,688]{0,1:T(8,128)(2,1)S(1)} fusion(bf16[2048,2048]{1,0:T(8,128)(2,1)} %gather_rows.3, bf16[2048,688]{0,1:T(8,128)(2,1)S(1)} %bitcast.42), kind=kOutput, calls=%fused_computation.13 | convolution fusion | flops 5772771328 | bytes 14024704 | tf_op jit(solution)/shard_map/dot_general | solution.py:22
  218.5 1.5 copy-done.29
  222.1 4.4 convolution_convert_fusion.3
  226.6 7.0 %convolution_convert_fusion.6 = bf16[344,2048]{1,0:T(8,128)(2,1)S(1)} fusion(bf16[2048,344]{0,1:T(8,128)(2,1)} %copy-done.31, bf16[2048,2048]{1,0:T(8,128)(2,1)} %get-tuple-element.73), kind=kOutput, calls=%fused_computation.23 | convolution fusion | flops 2886385664 | bytes 11206656 | tf_op jit(solution)/shard_map/dot_general | solution.py:30
  234.9 8.2 %fusion.7 = (bf16[2048,344]{0,1:T(8,128)(2,1)S(1)}, bf16[2048,344]{0,1:T(8,128)(2,1)S(1)}) fusion(bf16[2048,688]{0,1:T(8,128)(2,1)S(1)} %copy-done.30, bf16[2048,2048]{1,0:T(8,128)(2,1)} %get-tuple-element.73, bf16[344,2048]{1,0:T(8,128)(2,1)S(1)} %copy-done.47), kind=kOutput, calls=%fused_computation.20 | convolution fusion | flops 2896953344 | bytes 15433728 | tf_op jit(solution)/shard_map/dot_general | solution.py:26
  243.1 8.6 %convolution_convert_fusion.4.grad_gu_ref = bf16[2048,688]{1,0:T(8,128)(2,1)} fusion(bf16[2048,2048]{1,0:T(8,128)(2,1)S(1)} %bitcast.53, bf16[2048,344]{0,1:T(8,128)(2,1)S(1)} %get-tuple-element.133, bf16[2048,344]{0,1:T(8,128)(2,1)S(1)} %get-tuple-element.132), kind=kOutput, calls=%fused_computation.12 | convolution fusion | flops 5778407424 | bytes 14024704 | tf_op jit(solution)/shard_map/dot_general | solution.py:30
  251.8 7.2 %convolution_convert_fusion.part_ref = bf16[2048,2048]{1,0:T(8,128)(2,1)S(1)} fusion(bf16[2048,688]{0,1:T(8,128)(2,1)S(1)} %bitcast.43, bf16[2048,344]{0,1:T(8,128)(2,1)S(1)} %get-tuple-element.133, bf16[2048,344]{0,1:T(8,128)(2,1)S(1)} %get-tuple-element.132), kind=kOutput, calls=%fused_computation | convolution fusion | flops 5781192704 | bytes 14024704 | tf_op jit(solution)/shard_map/dot_general | solution.py:26
  259.0 58.1 %scatter_rows.1.d_norm_ref = f32[128,2048]{1,0:T(8,128)S(1)} custom-call(bf16[2048,2048]{1,0:T(8,128)(2,1)S(1)} %convolution_convert_fusion.part_ref), custom_call_target="tpu_custom_call" | custom-call | tf_op jit(solution)/shard_map/scatter_rows/pallas_call | solution.py:1506
  317.2 4.4 middle_backward.1
  324.2 10.2 %to_heads.1 = (bf16[2048,128]{1,0:T(8,128)(2,1)S(1)}, f32[16,8,128]{2,1,0:T(8,128)S(1)}) custom-call(bf16[128,2048]{1,0:T(8,128)(2,1)S(1)} %get-tuple-element.75.inner_ref, f32[16,8,128]{2,1,0:T(8,128)S(1)} %get-tuple-element.76.sums_ref), custom_call_target="tpu_custom_call" | custom-call | tf_op jit(solution)/shard_map/to_heads/pallas_call | solution.py:1695
  335.2 88.0 %inner_backward.1 = (bf16[2048,640]{1,0:T(8,128)(2,1)}, f32[1,128]{1,0:T(1,128)}, f32[64,128]{1,0:T(8,128)}, f32[64,128]{1,0:T(8,128)}, f32[64,128]{1,0:T(8,128)...) custom-call(s32[1,3]{1,0:T(1,128)} %starts_ref.3, ...), custom_call_target="tpu_custom_call" | custom-call | tf_op jit(solution)/shard_map/inner_backward/pallas_call | solution.py:622
  423.2 4.4 convolution_convert_fusion.2
  428.6 9.1 %fusion.24 = f32[2048,640]{0,1:T(8,128)S(1)} fusion(bf16[2048,2048]{1,0:T(8,128)(2,1)} %gather_rows.2.x_ref, bf16[2048,640]{1,0:T(8,128)(2,1)} %get-tuple-element.92), kind=kOutput, calls=%fused_computation.55 | convolution fusion | flops 5368709120 | bytes 16252928 | tf_op jit(solution)/shard_map/dot_general | solution.py:30
  437.7 2.3 copy-done.33
  440.5 2.5 copy.55.grad_in_ref
  445.0 5.1 convolution_convert_fusion.7.grad_out_ref
  450.3 9.3 %convolution_convert_fusion.1.part_ref = bf16[2048,2048]{1,0:T(8,128)(2,1)} fusion(bf16[2048,640]{1,0:T(8,128)(2,1)S(1)} %copy-done.45, bf16[2048,2]{1,0:T(8,128)(2,1)S(1)} %copy-done.34, bf16[2048,512]{1,0:T(8,128)(2,1)S(1)} %bitcast.55), kind=kOutput, calls=%fused_computation.1 | convolution fusion | flops 5380767744 | bytes 13115392 | tf_op jit(solution)/shard_map/dot_general | solution.py:26
  459.7 71.2 %scatter_rows_and_small.1 = (f32[128,2048]{1,0:T(8,128)S(1)}, f32[16,128]{1,0:T(8,128)S(1)}, f32[104,128]{1,0:T(8,128)S(1)}, f32[16,8,128]{2,1,0:T(8,128)S(1)}, ...) custom-call(bf16[2048,2048]{1,0:T(8,128)(2,1)} %convolution_convert_fusion.1.part_ref, ...), custom_call_target="tpu_custom_call" | custom-call | tf_op jit(solution)/shard_map/scatter_rows_and_small/pallas_call | solution.py:1522
  532.7 3.0 reshape.94
  541.8 5.2 copy.52
  547.0 3.4 slice_convert_fusion
  550.4 2.3 add_convert_fusion
  (161 shorter events, 29.9 us)
Async XLA Ops:
  7.2 202.7 %copy-start = (bf16[2048,2,344]{0,2,1:T(8,128)(2,1)S(1)}, bf16[2048,2,344]{0,2,1:T(8,128)(2,1)}, u32[]{:S(2)}) copy-start(bf16[2048,2,344]{0,2,1:T(8,128)(2,1)} %param.31) | copy-start | bytes 8454148
  7.2 144.3 %all-gather.2.cloned.1.call-start = ((), (), s32[]{:S(2)}) async-start(), calls=%async_computation.2 | async-start | bytes 8454144 | tf_op jit(solution)/shard_map/all_gather | solution.py:1747
  8.9 326.3 %reduce-scatter.3.cloned.1.call-start = ((), (), s32[]{:S(2)}) async-start(), calls=%async_computation.3 | async-start | bytes 4456448 | tf_op jit(solution)/shard_map/reduce_scatter | solution.py:1775
  70.3 62.5 %copy-start.42 = (f32[128]{0:T(128)S(1)}, f32[128]{0:T(128)}, u32[]{:S(2)}) copy-start(f32[128]{0:T(128)} %param.28) | copy-start | bytes 1540
  70.3 62.5 %copy-start.43 = (f32[128]{0:T(128)S(1)}, f32[128]{0:T(128)}, u32[]{:S(2)}) copy-start(f32[128]{0:T(128)} %param.27) | copy-start | bytes 1540
  82.2 50.7 %copy-start.3 = (bf16[2048,512]{1,0:T(8,128)(2,1)S(1)}, bf16[2048,512]{1,0:T(8,128)(2,1)}, u32[]{:S(2)}) copy-start(bf16[2048,512]{1,0:T(8,128)(2,1)} %get-tuple-element.64.proj_ref.gate_ref) | copy-start | bytes 6291460
  82.2 69.3 %copy-start.4 = (bf16[128,2048]{1,0:T(8,128)(2,1)S(1)}, bf16[128,2048]{1,0:T(8,128)(2,1)}, u32[]{:S(2)}) copy-start(bf16[128,2048]{1,0:T(8,128)(2,1)} %tokens_ref.3) | copy-start | bytes 1572868
  82.2 69.3 %copy-start.27 = (f32[2048]{0:T(1024)S(1)}, f32[2048]{0:T(1024)}, u32[]{:S(2)}) copy-start(f32[2048]{0:T(1024)} %param.30) | copy-start | bytes 24580
  226.5 323.9 %reduce-scatter.5.cloned.1.call-start = ((), (), s32[]{:S(2)}) async-start(), calls=%async_computation.4 | async-start | bytes 4456448 | tf_op jit(solution)/shard_map/reduce_scatter | solution.py:1824
  226.6 8.3 %copy-start.30 = (bf16[2048,688]{0,1:T(8,128)(2,1)S(1)}, bf16[2048,688]{0,1:T(8,128)(2,1)}, u32[]{:S(2)}) copy-start(bf16[2048,688]{0,1:T(8,128)(2,1)} %copy-done.29) | copy-start | bytes 8454148
  226.6 8.3 %copy-start.47 = (bf16[344,2048]{1,0:T(8,128)(2,1)S(1)}, bf16[344,2048]{1,0:T(8,128)(2,1)}, u32[]{:S(2)}) copy-start(bf16[344,2048]{1,0:T(8,128)(2,1)} %param.32) | copy-start | bytes 4227076
  233.6 9.5 %slice-start.2 = ((s8[8388608]{0:T(1024)(128)(4,1)}), s8[4194304]{0:T(1024)(128)(4,1)S(1)}, s32[]{:S(2)}) async-start(s8[8388608]{0:T(1024)(128)(4,1)} %bitcast.52), calls=%async_computation.7 | async-start | bytes 8388608
  234.9 8.3 %slice-start.3 = ((s8[8388608]{0:T(1024)(128)(4,1)}), s8[4194304]{0:T(1024)(128)(4,1)S(1)}, s32[]{:S(2)}) async-start(s8[8388608]{0:T(1024)(128)(4,1)} %bitcast.52), calls=%async_computation.8 | async-start | bytes 8388608
  243.1 74.0 %slice-start = ((s8[8388608]{0:T(1024)(128)(4,1)}), s8[4194304]{0:T(1024)(128)(4,1)S(1)}, s32[]{:S(2)}) async-start(s8[8388608]{0:T(1024)(128)(4,1)} %bitcast.45), calls=%async_computation.5 | async-start | bytes 8388608
  251.8 65.4 %slice-start.1 = ((s8[8388608]{0:T(1024)(128)(4,1)}), s8[4194304]{0:T(1024)(128)(4,1)S(1)}, s32[]{:S(2)}) async-start(s8[8388608]{0:T(1024)(128)(4,1)} %bitcast.45), calls=%async_computation.6 | async-start | bytes 8388608
  259.0 58.2 %copy-start.6 = (f32[128,2048]{1,0:T(8,128)S(1)}, f32[128,2048]{1,0:T(8,128)}, u32[]{:S(2)}) copy-start(f32[128,2048]{1,0:T(8,128)} %copy-done.5) | copy-start | bytes 3145732
  259.0 58.2 %copy-start.7 = (bf16[128,2048]{1,0:T(8,128)(2,1)S(1)}, bf16[128,2048]{1,0:T(8,128)(2,1)}, u32[]{:S(2)}) copy-start(bf16[128,2048]{1,0:T(8,128)(2,1)} %cot_ref.3) | copy-start | bytes 1572868
  259.0 58.2 %copy-start.10 = (bf16[128,2048]{1,0:T(8,128)(2,1)S(1)}, bf16[128,2048]{1,0:T(8,128)(2,1)}, u32[]{:S(2)}) copy-start(bf16[128,2048]{1,0:T(8,128)(2,1)} %copy-done.8) | copy-start | bytes 1572868
  259.0 58.2 %copy-start.13 = (bf16[128,2048]{1,0:T(8,128)(2,1)S(1)}, bf16[128,2048]{1,0:T(8,128)(2,1)}, u32[]{:S(2)}) copy-start(bf16[128,2048]{1,0:T(8,128)(2,1)} %copy-done.11) | copy-start | bytes 1572868
  335.2 88.0 %copy-start.32 = (bf16[2048,344]{0,1:T(8,128)(2,1)S(1)}, bf16[2048,344]{0,1:T(8,128)(2,1)}, u32[]{:S(2)}) copy-start(bf16[2048,344]{0,1:T(8,128)(2,1)} %copy-done.31) | copy-start | bytes 4227076
  335.2 88.0 %copy-start.48 = (bf16[344,2048]{1,0:T(8,128)(2,1)S(1)}, bf16[344,2048]{1,0:T(8,128)(2,1)}, u32[]{:S(2)}) copy-start(bf16[344,2048]{1,0:T(8,128)(2,1)} %param.32) | copy-start | bytes 4227076
  428.6 9.1 %copy-start.41 = (f32[8,128]{1,0:T(8,128)}, f32[8,128]{1,0:T(8,128)S(1)}, u32[]{:S(2)}) copy-start(f32[8,128]{1,0:T(8,128)S(1)} %reduce_sum.46) | copy-start | bytes 12292
  440.4 4.3 copy-start.40
  440.4 4.5 copy-start.39
  440.5 4.5 slice-start.4
  440.5 4.5 copy-start.44
  445.0 5.2 copy-start.28
  445.0 5.2 copy-start.34
  445.0 5.3 copy-start.45
  450.3 9.3 %copy-start.15 = (f32[128,2048]{1,0:T(8,128)S(1)}, f32[128,2048]{1,0:T(8,128)}, u32[]{:S(2)}) copy-start(f32[128,2048]{1,0:T(8,128)} %copy-done.14) | copy-start | bytes 3145732
  450.3 9.3 %copy-start.26 = (f32[2048]{0:T(1024)S(1)}, f32[2048]{0:T(1024)}, u32[]{:S(2)}) copy-start(f32[2048]{0:T(1024)} %param.19) | copy-start | bytes 24580
  547.0 7.2 %copy-start.1 = (bf16[2048,2,344]{0,2,1:T(8,128)(2,1)S(1)}, bf16[2048,2,344]{0,2,1:T(8,128)(2,1)}, u32[]{:S(2)}) copy-start(bf16[2048,2,344]{0,2,1:T(8,128)(2,1)} %param.31) | copy-start | bytes 8454148
  (26 other events, 46.1 us)
Sparse Core Ops, SparseCore 0:
  11.7 75.7 all-gather.1
  226.6 83.7 reduce-scatter.2
  427.7 77.5 reduce-scatter.4

commit v2 on v1

--- a/solution.py
+++ b/solution.py
@@ -304,8 +304,7 @@
     dinner_ref,
     dgate_ref,
     mixed_ref,
-    grad_gu_ref,
-    grad_down_ref,
+    grads_ref,
     mix_ref,
     z_ref,
     g_ref,
@@ -335,8 +334,7 @@
     dz_ref,
     lam_ref,
     mixed_out,
-    sum_gu_ref,
-    sum_down_ref,
+    sums_ref,
     mix_rows_ref,
     head_ref,
     earlier_ref,
@@ -346,18 +344,14 @@
     *sems,
 ):
     chunks = rate_ref.shape[0]
-    gather = Gather(mix_ref, mix_rows_ref, *sems[2 * SEQ_SUM_SCRATCH :])
-    sums = (
-        SeqSum(0, grad_gu_ref, sum_gu_ref, *sems[:SEQ_SUM_SCRATCH]),
-        SeqSum(1, grad_down_ref, sum_down_ref, *sems[SEQ_SUM_SCRATCH : 2 * SEQ_SUM_SCRATCH]),
-    )
+    gather = Gather(mix_ref, mix_rows_ref, *sems[SEQ_SUM_SCRATCH:])
+    total = SeqSum(1, grads_ref, sums_ref, *sems[:SEQ_SUM_SCRATCH])
     exchange = ToHeads(
         [(dgate_ref, dproj_ref, 3 * LANES), (mixed_ref, mixed_out, 0)], send_sem, recv_sem
     )
-    gather.start([{"head": peer} for peer in exchange.peers] + sums[0].peers())
+    gather.start([{"head": peer} for peer in exchange.peers] + total.peers())
     exchange.start()
-    for total in sums:
-        total.start()
+    total.start()
     places = Places(starts_ref)
     inner_masks(head_ref, earlier_ref, output_ref)
     dbias_ref[...] = jnp.zeros_like(dbias_ref)
@@ -529,8 +523,7 @@
         for step, when in enumerate(BACKWARD_STEPS):
             pl.when(index == when)(gather.steps[step])
         for step, when in enumerate(SUM_STEPS):
-            for total in sums:
-                pl.when(index == when)(total.steps[step])
+            pl.when(index == when)(total.steps[step])
         after = wrap(chunk + 1, chunks)
         cross = mx_ref[chunk + 1]
         dz = chain(chunk, dz_after, cross)
@@ -564,8 +557,7 @@
     dc_ref[...] += lam_c + add_c
     finish(0)
     exchange.end()
-    for total in sums:
-        total.end()
+    total.end()
     gather.end()
 
 
@@ -640,28 +632,27 @@
             cell16,
             cell,
             jax.ShapeDtypeStruct((tokens, LANES), BF16),
-            *(jax.ShapeDtypeStruct(grad.shape, BF16) for grad in grads),
+            jax.ShapeDtypeStruct(grads.shape, BF16),
             gathered_shape(own),
         ],
         in_specs=[pl.BlockSpec(memory_space=pltpu.SMEM)]
-        + whole_vmem(7)
+        + whole_vmem(6)
         + [ANYWHERE]
         + whole_vmem(len(kept)),
-        out_specs=whole_vmem(20) + [ANYWHERE],
+        out_specs=whole_vmem(19) + [ANYWHERE],
         scratch_shapes=[
             pltpu.VMEM((LANES, LANES), F32),
             pltpu.VMEM((LANES, LANES), F32),
             pltpu.VMEM((LANES, LANES), F32),
         ]
         + to_heads_scratch(2)
-        + seq_sum_scratch(grads[0].shape, 0)
-        + seq_sum_scratch(grads[1].shape, 1)
+        + seq_sum_scratch(grads.shape, 1)
         + gather_scratch(),
         compiler_params=pltpu.CompilerParams(
             collective_id=number, has_side_effects=True, vmem_limit_bytes=MOST_VMEM
         ),
         name="inner_backward",
-    )(starts, proj, rates, d_inner, d_gate, mixed, *grads, own, *kept)
+    )(starts, proj, rates, d_inner, d_gate, mixed, grads, own, *kept)
 
 
 def heads_of_lanes(values):
@@ -1314,8 +1305,66 @@
 EVERYWHERE_SCRATCH = 7
 
 
-def scatter_kernel(part_ref, sum_ref, held_ref, stage_ref, send_sem, recv_sem):
-    scatter_body(None, part_ref, sum_ref, held_ref, stage_ref, send_sem, recv_sem)
+class FeedForwardGradients:
+    def __init__(self, turned, rows_ref, cot_ref, grads_ref, wide_ref, sem):
+        self.turned, self.grads_ref, self.wide_ref = turned, grads_ref, wide_ref
+        self.fetch = pltpu.make_async_copy(rows_ref, wide_ref, sem.at[0])
+        self.fetch_cot = pltpu.make_async_copy(cot_ref, wide_ref, sem.at[1])
+        self.padded = grads_ref.shape[0] // len(turned)
+        self.tile = 256
+        self.tiles = wide_ref.shape[1] // self.tile
+
+    def start(self):
+        self.fetch.start()
+
+    def product(self, indices, first, last):
+        def step(number, carry):
+            cut = pl.ds(pl.multiple_of(number * self.tile, self.tile), self.tile)
+            wide = self.wide_ref[:, cut]
+            for index in indices:
+                turned = self.turned[index]
+                spare = jnp.zeros((self.padded - turned.shape[0], self.tile), F32)
+                product = jnp.concatenate([dot_nn(turned[...], wide), spare], axis=0)
+                place = slice(index * self.padded, (index + 1) * self.padded)
+                self.grads_ref[place, cut] = product.astype(BF16)
+            return carry
+
+        lax.fori_loop(first, last, step, 0)
+
+    def piece(self, index):
+        half = self.tiles // 2
+        if index == 0:
+            self.fetch.wait()
+            self.product((0, 1), 0, half)
+        elif index == 1:
+            self.product((0, 1), half, self.tiles)
+            self.fetch_cot.start()
+        elif index == 2:
+            self.fetch_cot.wait()
+            self.product((2,), 0, self.tiles)
+
+
+def scatter_kernel(
+    part_ref,
+    d_gate_ref,
+    d_up_ref,
+    hidden_ref,
+    rows_ref,
+    cot_ref,
+    sum_ref,
+    grads_ref,
+    held_ref,
+    stage_ref,
+    send_sem,
+    recv_sem,
+    wide_ref,
+    sem,
+):
+    work = FeedForwardGradients(
+        (d_gate_ref, d_up_ref, hidden_ref), rows_ref, cot_ref, grads_ref, wide_ref, sem
+    )
+    work.start()
+    scatter_body(None, part_ref, sum_ref, held_ref, stage_ref, send_sem, recv_sem, work)
 
 
 def scatter_small_kernel(
@@ -1366,7 +1415,9 @@
     gain_sum.end()
 
 
-def scatter_body(small, part_ref, sum_ref, held_ref, stage_ref, send_sem, recv_sem):
+def scatter_body(
+    small, part_ref, sum_ref, held_ref, stage_ref, send_sem, recv_sem, work=None
+):
     head = lax.axis_index("head")
     near = neighbours(head)
     rows = sum_ref.shape[0]
@@ -1451,11 +1502,15 @@
     if small is not None:
         small.start()
         small.step(0)
+    if work is not None:
+        work.piece(0)
     onwards = {
         (axis, o): onward(axis, units, o, fars[axis, o]) for o in order for axis, units in halves
     }
     if small is not None:
         small.step(1)
+    if work is not None:
+        work.piece(1)
     last_far, last_plain, last_onward = {}, {}, {}
 
     def first_sum(axis, units, other):
@@ -1473,6 +1528,8 @@
         last_plain[axis] = plain(1 - axis, units, 0)
     if small is not None:
         small.step(2)
+    if work is not None:
+        work.piece(2)
     for axis, units in halves:
         last_onward[axis] = onward(1 - axis, units, 0, last_far[axis])
     if small is not None:
@@ -1501,19 +1558,25 @@
     ]
 
 
-def scatter_rows(part, number):
+def scatter_rows(part, turned, rows_all, cot_rows, number):
     rows, width = part.shape[0] // GROUP, part.shape[1]
+    columns, tokens = turned[0].shape
+    padded = columns + -columns % 16
     return pl.pallas_call(
         scatter_kernel,
-        out_shape=jax.ShapeDtypeStruct((rows, width), F32),
-        in_specs=[pl.BlockSpec(memory_space=pltpu.VMEM)],
-        out_specs=pl.BlockSpec(memory_space=pltpu.VMEM),
-        scratch_shapes=scatter_scratch(rows, width),
+        out_shape=[
+            jax.ShapeDtypeStruct((rows, width), F32),
+            jax.ShapeDtypeStruct((len(turned) * padded, width), BF16),
+        ],
+        in_specs=whole_vmem(1 + len(turned)) + [ANYWHERE, ANYWHERE],
+        out_specs=whole_vmem(2),
+        scratch_shapes=scatter_scratch(rows, width)
+        + [pltpu.VMEM((tokens, width), BF16), pltpu.SemaphoreType.DMA((2,))],
         compiler_params=pltpu.CompilerParams(
-            collective_id=number, has_side_effects=True, vmem_limit_bytes=28 * 1024 * 1024
+            collective_id=number, has_side_effects=True, vmem_limit_bytes=44 * 1024 * 1024
         ),
         name="scatter_rows",
-    )(part)
+    )(part, *turned, rows_all, cot_rows)
 
 
 def scatter_rows_and_small(part, shard, grads, tokens, d_res, gain, seqs, number):
@@ -1775,13 +1838,13 @@
     out_first = lax.psum_scatter(ffn_first, "head", scatter_dimension=0, tiled=True)
     cot_rows = after(cot_rows, ffn_first)
     d_hidden = dot_nt(cot_rows, w_down)
-    d_gate_part = silu_pull(d_hidden * up_part)[0]
-    d_gate_up = jnp.concatenate([d_gate_part, d_hidden * silu_val], axis=1).astype(BF16)
-    grad_w_down = dot_tn(hidden_state, cot_rows).astype(BF16)
-    grad_w_down = jnp.pad(grad_w_down, ((0, -ffn_local % 16), (0, 0)))
-    grad_w_gate_up = dot_tn(ffn_rows, d_gate_up).astype(BF16)
+    d_gate_part = silu_pull(d_hidden * up_part)[0].astype(BF16)
+    d_up_part = (d_hidden * silu_val).astype(BF16)
+    d_gate_up = jnp.concatenate([d_gate_part, d_up_part], axis=1)
     d_norm_part = dot_nt(d_gate_up, w_gu_flat).astype(BF16)
-    d_norm_two = scatter_rows(after(d_norm_part, grad_w_down, grad_w_gate_up), 3)
+    d_norm_two, ffn_grads = scatter_rows(
+        d_norm_part, (d_gate_part.T, d_up_part.T, hidden_state.T), ffn_rows, cot_rows, 3
+    )
 
     d_res, d_mix, d_inner_tok, d_gate_tok, token_sums = middle_backward(
         d_norm_two,
@@ -1805,8 +1868,7 @@
         d_shift,
         *_,
         mixed_in,
-        sum_w_gate_up,
-        sum_w_down,
+        ffn_sums,
         mix_rows,
     ) = inner_backward(
         doc_starts,
@@ -1815,11 +1877,12 @@
         after(d_inner, out_first),
         d_gate_tok,
         mixed_tok,
-        (grad_w_gate_up, grad_w_down),
+        ffn_grads,
         d_mix,
         kept,
         8,
     )
+    ffn_sums = ffn_sums.reshape(3, -1, width)[:, :ffn_local].astype(F32)
     ffn_second = dot_nn(after(hidden_state, d_projected), w_down[:, half:]).astype(BF16)
     out_second = lax.psum_scatter(ffn_second, "head", scatter_dimension=0, tiled=True)
     ffn_out = jnp.concatenate([out_first, out_second], axis=1).astype(F32)
@@ -1873,8 +1936,8 @@
         shard[2],
         sum_w_out.astype(F32),
         sum_ffn_gain,
-        sum_w_gate_up.astype(F32).reshape(width, 2, ffn_local),
-        sum_w_down[:ffn_local].astype(F32),
+        ffn_sums[:2].transpose(2, 0, 1),
+        ffn_sums[2],
     )
 
 

time: 570 us -> 573 us (level)
  matrix products: 72.1 us -> 57.9 us
  Pallas kernels: 414 us -> 426 us
    dot_general x4 -> x2, matrix products: 29.8 us -> 14.6 us  [dot_tn(): lax.dot_general(a, b, (((0,), (0,)), ((), ())), preferred_element_type=F32)]
    pallas_call x1, Pallas kernels: 58.1 us -> 64.8 us  [scatter_rows(): pl.pallas_call(scatter_kernel, out_shape=[jax.ShapeDtypeStruct((rows, wid...]
    unnamed x113 -> x115, local copies, waits for them, and re-layouts: 29.5 us -> 34.4 us
  transfers between devices with their start and end apart: 3 -> 3, of which waited for: 0 -> 0; matrix products, arithmetic and copies ran while one was open for 16% -> 13% of each run, Pallas kernels for 49% -> 51%
where the time goes in v2:
time: 573 us; the launch traced here: 564 us
  Pallas kernels  426 us (74%)
  matrix products  57.9 us (10%)
  local copies, waits for them, and re-layouts  52.1 us (9%)
  between operations  14.8 us (3%)
  other arithmetic  13.6 us (2%)
    pallas_call x2, Pallas kernels, gather_rows(): pl.pallas_call(gather_kernel, out_shape=gathered_shape(own), in_specs=[AN...  104 us
    pallas_call x1, Pallas kernels, inner_backward(): pl.pallas_call(backward_kernel, out_shape=[jax.ShapeDtypeStruct((tokens,...  87.4 us
    pallas_call x1, Pallas kernels, scatter_rows_and_small(): pl.pallas_call(scatter_small_kernel, out_shape=[jax.ShapeDtypeStruct((row...  73.1 us
    pallas_call x1, Pallas kernels, scatter_rows(): pl.pallas_call(scatter_kernel, out_shape=[jax.ShapeDtypeStruct((rows, wid...  64.8 us
    pallas_call x1, Pallas kernels, inner_forward(): pl.pallas_call(forward_kernel, out_shape=[jax.ShapeDtypeStruct((tokens, L...  52.2 us
    unnamed x115, local copies, waits for them, and re-layouts  34.4 us
    dot_general x3, matrix products, dot_nt(): lax.dot_general(a, b, (((1,), (1,)), ((), ())), preferred_element_type=F32)  25.9 us
    dot_general x3, matrix products, dot_nn(): lax.dot_general(a, b, (((1,), (0,)), ((), ())), preferred_element_type=F32)  17.5 us
  transfers between devices with their start and end apart: 3, of which 0 were waited for; matrix products, arithmetic and copies ran while one was open for 13% of the time, Pallas kernels for 51%

profile of v2, /device:TPU:1, one launch (start us, length us, event | category | flops | bytes accessed | tf_op | source)
XLA Modules:
  0.0 564.2 jit_solution(11417742492231754452)
XLA Ops:
  7.3 1.6 constant_dynamic-slice_fusion
  10.3 3.3 copy.47
  14.8 53.4 %gather_rows.2.x_ref = bf16[2048,2048]{1,0:T(8,128)(2,1)} custom-call(bf16[128,2048]{1,0:T(8,128)(2,1)} %fusion.19.refs_0_), custom_call_target="tpu_custom_call" | custom-call | tf_op jit(solution)/shard_map/gather_rows/pallas_call | solution.py:1003
  68.9 11.7 %project.1 = (bf16[2048,512]{1,0:T(8,128)(2,1)}, f32[32,1,128]{2,1,0:T(1,128)}) custom-call(bf16[2048,2048]{1,0:T(8,128)(2,1)} %gather_rows.2.x_ref, bf16[2048,512]{1,0:T(8,128)(2,1)} %bitcast.59, bf16[16,2048]{1,0:T(8,128)(2,1)} %pad.8.rate_w_ref, f32[1,128]{1,0:T(1,128)} %broadcast_in_dim_reshape.3.bias_ref), custom_call_target="tpu_custom_call" | custom-call | tf_op jit(solution)/shard_map/project/pallas_call | solution.py:678
  80.7 52.2 %inner_forward.1 = (bf16[2048,128]{1,0:T(8,128)(2,1)}, f32[32,64,128]{2,1,0:T(8,128)}, f32[32,64,128]{2,1,0:T(8,128)}, f32[32,64,128]{2,1,0:T(8,128)}, f32[33,64...) custom-call(s32[1,3]{1,0:T(1,128)} %starts_ref.3, ...), custom_call_target="tpu_custom_call" | custom-call | tf_op jit(solution)/shard_map/inner_forward/pallas_call | solution.py:573
  134.0 16.1 %to_tokens.1 = (bf16[128,2048]{1,0:T(8,128)(2,1)S(1)}, bf16[128,2048]{1,0:T(8,128)(2,1)S(1)}, f32[16,8,128]{2,1,0:T(8,128)S(1)}) custom-call(bf16[2048,128]{1,0:T(8,128)(2,1)S(1)} %copy-done.28, bf16[2048,512]{1,0:T(8,128)(2,1)S(1)} %copy-done.3, f32[8,128]{1,0:T(8,128)S(1)} %maximum_maximum_fusion.gains_ref), custom_call_target="tpu_custom_call" | custom-call | tf_op jit(solution)/shard_map/to_tokens/pallas_call | solution.py:1672
  151.7 3.4 copy-done.2
  157.2 1.9 middle_forward.1
  161.7 50.6 %gather_rows.3.rows_ref = bf16[2048,2048]{1,0:T(8,128)(2,1)} custom-call(bf16[128,2048]{1,0:T(8,128)(2,1)} %copy-done.29), custom_call_target="tpu_custom_call" | custom-call | tf_op jit(solution)/shard_map/gather_rows/pallas_call | solution.py:1003
  212.4 8.7 %convolution_convert_fusion.4 = bf16[2048,688]{0,1:T(8,128)(2,1)S(1)} fusion(bf16[2048,2048]{1,0:T(8,128)(2,1)} %gather_rows.3.rows_ref, bf16[2048,688]{0,1:T(8,128)(2,1)S(1)} %bitcast.47), kind=kOutput, calls=%fused_computation.14 | convolution fusion | flops 5772771328 | bytes 14024704 | tf_op jit(solution)/shard_map/dot_general | solution.py:22
  224.7 4.4 convolution_convert_fusion.3
  229.2 2.9 fusion.39.hidden_ref
  232.2 7.5 %fusion.7 = (bf16[2048,344]{0,1:T(8,128)(2,1)S(1)}, bf16[2048,344]{0,1:T(8,128)(2,1)S(1)}) fusion(bf16[2048,688]{0,1:T(8,128)(2,1)S(1)} %copy-done.33, bf16[2048,2048]{1,0:T(8,128)(2,1)} %get-tuple-element.73.cot_ref, bf16[344,2048]{1,0:T(8,128)(2,1)S(1)} %copy-done.51), kind=kOutput, calls=%fused_computation.21 | convolution fusion | flops 2896953344 | bytes 15433728 | tf_op jit(solution)/shard_map/dot_general | solution.py:26
  239.8 9.1 %convolution_convert_fusion.part_ref = bf16[2048,2048]{1,0:T(8,128)(2,1)} fusion(bf16[2048,688]{0,1:T(8,128)(2,1)S(1)} %bitcast.48, bf16[2048,344]{0,1:T(8,128)(2,1)S(1)} %get-tuple-element.117, bf16[2048,344]{0,1:T(8,128)(2,1)S(1)} %get-tuple-element.116), kind=kOutput, calls=%fused_computation | convolution fusion | flops 5781192704 | bytes 14024704 | tf_op jit(solution)/shard_map/dot_general | solution.py:26
  250.4 1.7 copy-done.18
  252.2 64.8 %scatter_rows.1 = (f32[128,2048]{1,0:T(8,128)S(1)}, bf16[1056,2048]{1,0:T(8,128)(2,1)S(1)}) custom-call(bf16[2048,2048]{1,0:T(8,128)(2,1)} %convolution_convert_fusion.part_ref, bf16[344,2048]{1,0:T(8,128)(2,1)S(1)} %bitcast.53, bf16[344,2048]{1,0:T(8,128)(2,1)S(1)} %bitcast.54, bf16[344,2048]{1,0:T(8,128)(2,1)S(1)} %fusion.39.hidden_ref, ...), custom_call_target="tpu_custom_call" | custom-call | tf_op jit(solution)/shard_map/scatter_rows/pallas_call | solution.py:1565
  318.5 4.3 middle_backward.1
  325.4 10.0 %to_heads.1 = (bf16[2048,128]{1,0:T(8,128)(2,1)S(1)}, f32[16,8,128]{2,1,0:T(8,128)S(1)}) custom-call(bf16[128,2048]{1,0:T(8,128)(2,1)S(1)} %get-tuple-element.75.inner_ref, f32[16,8,128]{2,1,0:T(8,128)S(1)} %get-tuple-element.76.sums_ref), custom_call_target="tpu_custom_call" | custom-call | tf_op jit(solution)/shard_map/to_heads/pallas_call | solution.py:1758
  336.2 87.4 %inner_backward.1 = (bf16[2048,640]{1,0:T(8,128)(2,1)}, f32[1,128]{1,0:T(1,128)}, f32[64,128]{1,0:T(8,128)}, f32[64,128]{1,0:T(8,128)}, f32[64,128]{1,0:T(8,128)...) custom-call(s32[1,3]{1,0:T(1,128)} %starts_ref.3, ...), custom_call_target="tpu_custom_call" | custom-call | tf_op jit(solution)/shard_map/inner_backward/pallas_call | solution.py:614
  423.6 4.4 convolution_convert_fusion.2
  430.2 9.3 %fusion.26 = f32[2048,640]{0,1:T(8,128)S(1)} fusion(bf16[2048,2048]{1,0:T(8,128)(2,1)} %gather_rows.2.x_ref, bf16[2048,640]{1,0:T(8,128)(2,1)} %get-tuple-element.93), kind=kOutput, calls=%fused_computation.56 | convolution fusion | flops 5368709120 | bytes 16252928 | tf_op jit(solution)/shard_map/dot_general | solution.py:30
  439.5 2.3 copy-done.37
  442.2 2.5 copy.44.grad_in_ref
  445.7 5.3 convolution_convert_fusion.5.grad_out_ref
  451.1 9.3 %convolution_convert_fusion.1.part_ref = bf16[2048,2048]{1,0:T(8,128)(2,1)} fusion(bf16[2048,640]{1,0:T(8,128)(2,1)S(1)} %copy-done.49, bf16[2048,2]{1,0:T(8,128)(2,1)S(1)} %copy-done.38, bf16[2048,512]{1,0:T(8,128)(2,1)S(1)} %bitcast.60), kind=kOutput, calls=%fused_computation.1 | convolution fusion | flops 5380767744 | bytes 13115392 | tf_op jit(solution)/shard_map/dot_general | solution.py:26
  460.4 73.1 %scatter_rows_and_small.1 = (f32[128,2048]{1,0:T(8,128)S(1)}, f32[16,128]{1,0:T(8,128)S(1)}, f32[104,128]{1,0:T(8,128)S(1)}, f32[16,8,128]{2,1,0:T(8,128)S(1)}, ...) custom-call(bf16[2048,2048]{1,0:T(8,128)(2,1)} %convolution_convert_fusion.1.part_ref, ...), custom_call_target="tpu_custom_call" | custom-call | tf_op jit(solution)/shard_map/scatter_rows_and_small/pallas_call | solution.py:1585
  540.4 2.1 convert_element_type.72
  542.5 2.9 reshape.90
  545.5 3.3 slice_convert_fusion
  548.8 1.8 slice_bitcast_fusion.1
  550.5 2.9 slice_bitcast_fusion
  553.4 2.3 add_convert_fusion
  (161 shorter events, 32.9 us)
Async XLA Ops:
  7.2 205.2 %copy-start = (bf16[2048,2,344]{0,2,1:T(8,128)(2,1)S(1)}, bf16[2048,2,344]{0,2,1:T(8,128)(2,1)}, u32[]{:S(2)}) copy-start(bf16[2048,2,344]{0,2,1:T(8,128)(2,1)} %param.31) | copy-start | bytes 8454148
  7.2 6.4 %copy-start.4 = (bf16[128,2048]{1,0:T(8,128)(2,1)S(1)}, bf16[128,2048]{1,0:T(8,128)(2,1)}, u32[]{:S(2)}) copy-start(bf16[128,2048]{1,0:T(8,128)(2,1)} %tokens_ref.3) | copy-start | bytes 1572868
  7.2 6.6 %copy-start.30 = (f32[2048]{0:T(1024)S(1)}, f32[2048]{0:T(1024)}, u32[]{:S(2)}) copy-start(f32[2048]{0:T(1024)} %param.19) | copy-start | bytes 24580
  7.2 144.5 %all-gather.2.cloned.1.call-start = ((), (), s32[]{:S(2)}) async-start(), calls=%async_computation.2 | async-start | bytes 8454144 | tf_op jit(solution)/shard_map/all_gather | solution.py:1810
  8.9 327.3 %reduce-scatter.3.cloned.1.call-start = ((), (), s32[]{:S(2)}) async-start(), calls=%async_computation.3 | async-start | bytes 4456448 | tf_op jit(solution)/shard_map/reduce_scatter | solution.py:1838
  14.8 53.5 %copy-start.40 = (bf16[2048,2]{0,1:T(2,128)(2,1)S(1)}, bf16[2048,2]{0,1:T(2,128)(2,1)}, u32[]{:S(2)}) copy-start(bf16[2048,2]{0,1:T(2,128)(2,1)} %param.21) | copy-start | bytes 24580
  68.9 64.0 %copy-start.46 = (f32[128]{0:T(128)S(1)}, f32[128]{0:T(128)}, u32[]{:S(2)}) copy-start(f32[128]{0:T(128)} %param.28) | copy-start | bytes 1540
  68.9 64.0 %copy-start.47 = (f32[128]{0:T(128)S(1)}, f32[128]{0:T(128)}, u32[]{:S(2)}) copy-start(f32[128]{0:T(128)} %param.27) | copy-start | bytes 1540
  80.7 52.3 %copy-start.3 = (bf16[2048,512]{1,0:T(8,128)(2,1)S(1)}, bf16[2048,512]{1,0:T(8,128)(2,1)}, u32[]{:S(2)}) copy-start(bf16[2048,512]{1,0:T(8,128)(2,1)} %get-tuple-element.64.proj_ref.gate_ref) | copy-start | bytes 6291460
  80.7 71.1 %copy-start.31 = (f32[2048]{0:T(1024)S(1)}, f32[2048]{0:T(1024)}, u32[]{:S(2)}) copy-start(f32[2048]{0:T(1024)} %param.30) | copy-start | bytes 24580
  151.7 3.4 copy-start.2
  229.1 324.3 %reduce-scatter.5.cloned.1.call-start = ((), (), s32[]{:S(2)}) async-start(), calls=%async_computation.4 | async-start | bytes 4456448 | tf_op jit(solution)/shard_map/reduce_scatter | solution.py:1887
  229.2 3.0 copy-start.51
  239.8 9.1 %copy-start.15 = (bf16[2048,344]{0,1:T(8,128)(2,1)}, bf16[2048,344]{0,1:T(8,128)(2,1)S(1)}, u32[]{:S(2)}) copy-start(bf16[2048,344]{0,1:T(8,128)(2,1)S(1)} %get-tuple-element.116) | copy-start | bytes 4227076
  239.8 9.1 %copy-start.17 = (bf16[2048,344]{0,1:T(8,128)(2,1)}, bf16[2048,344]{0,1:T(8,128)(2,1)S(1)}, u32[]{:S(2)}) copy-start(bf16[2048,344]{0,1:T(8,128)(2,1)S(1)} %get-tuple-element.117) | copy-start | bytes 4227076
  248.9 68.2 %slice-start = ((s8[8388608]{0:T(1024)(128)(4,1)}), s8[4194304]{0:T(1024)(128)(4,1)S(1)}, s32[]{:S(2)}) async-start(s8[8388608]{0:T(1024)(128)(4,1)} %bitcast.50), calls=%async_computation.5 | async-start | bytes 8388608
  252.2 64.9 %slice-start.1 = ((s8[8388608]{0:T(1024)(128)(4,1)}), s8[4194304]{0:T(1024)(128)(4,1)S(1)}, s32[]{:S(2)}) async-start(s8[8388608]{0:T(1024)(128)(4,1)} %bitcast.50), calls=%async_computation.6 | async-start | bytes 8388608
  252.2 64.9 %copy-start.7 = (f32[128,2048]{1,0:T(8,128)S(1)}, f32[128,2048]{1,0:T(8,128)}, u32[]{:S(2)}) copy-start(f32[128,2048]{1,0:T(8,128)} %copy-done.6) | copy-start | bytes 3145732
  252.2 64.9 %copy-start.8 = (bf16[128,2048]{1,0:T(8,128)(2,1)S(1)}, bf16[128,2048]{1,0:T(8,128)(2,1)}, u32[]{:S(2)}) copy-start(bf16[128,2048]{1,0:T(8,128)(2,1)} %cot_ref.3) | copy-start | bytes 1572868
  252.2 64.9 %copy-start.11 = (bf16[128,2048]{1,0:T(8,128)(2,1)S(1)}, bf16[128,2048]{1,0:T(8,128)(2,1)}, u32[]{:S(2)}) copy-start(bf16[128,2048]{1,0:T(8,128)(2,1)} %copy-done.9) | copy-start | bytes 1572868
  317.0 5.8 %copy-start.5 = (bf16[1056,2048]{1,0:T(8,128)(2,1)}, bf16[1056,2048]{1,0:T(8,128)(2,1)S(1)}, u32[]{:S(2)}) copy-start(bf16[1056,2048]{1,0:T(8,128)(2,1)S(1)} %get-tuple-element.81.grads_ref) | copy-start | bytes 12976132
  336.2 87.4 %copy-start.36 = (bf16[2048,344]{0,1:T(8,128)(2,1)S(1)}, bf16[2048,344]{0,1:T(8,128)(2,1)}, u32[]{:S(2)}) copy-start(bf16[2048,344]{0,1:T(8,128)(2,1)} %copy-done.35) | copy-start | bytes 4227076
  336.2 87.4 %copy-start.52 = (bf16[344,2048]{1,0:T(8,128)(2,1)S(1)}, bf16[344,2048]{1,0:T(8,128)(2,1)}, u32[]{:S(2)}) copy-start(bf16[344,2048]{1,0:T(8,128)(2,1)} %param.32) | copy-start | bytes 4227076
  429.1 10.4 %copy-start.45 = (f32[8,128]{1,0:T(8,128)}, f32[8,128]{1,0:T(8,128)S(1)}, u32[]{:S(2)}) copy-start(f32[8,128]{1,0:T(8,128)S(1)} %reduce_sum.46) | copy-start | bytes 12292
  442.2 3.4 copy-start.43
  442.2 3.4 slice-start.2
  442.2 3.4 copy-start.48
  445.7 5.3 copy-start.34
  445.7 5.3 copy-start.38
  445.7 5.4 copy-start.49
  451.1 9.3 %copy-start.20 = (f32[128,2048]{1,0:T(8,128)S(1)}, f32[128,2048]{1,0:T(8,128)}, u32[]{:S(2)}) copy-start(f32[128,2048]{1,0:T(8,128)} %copy-done.19) | copy-start | bytes 3145732
  550.5 6.7 %copy-start.1 = (bf16[2048,2,344]{0,2,1:T(8,128)(2,1)S(1)}, bf16[2048,2,344]{0,2,1:T(8,128)(2,1)}, u32[]{:S(2)}) copy-start(bf16[2048,2,344]{0,2,1:T(8,128)(2,1)} %param.31) | copy-start | bytes 8454148
  (27 other events, 36.7 us)
Sparse Core Ops, SparseCore 0:
  11.8 75.8 all-gather.1
  229.3 82.2 reduce-scatter.2
  428.2 79.3 reduce-scatter.4
